TPU v7x, 256 devices: a whole 4x4x8 slice. The times are simulated.
256 devices in a mesh: img: 16 (over z_lo, x, core), ref: 16 (over z_hi, y).
Axes of the slice: x: 4, y: 4, z: 8 (z_hi: 4, z_lo: 2; z = z_hi * 2 + z_lo), core: 2. Of those that a mesh axis runs over, the one named last changes fastest.
Arguments:
- images: bfloat16 [8192, 16384], P('img', 'ref'), may hold values from -24 to 24
- refs: bfloat16 [6912, 16384], P('ref', 'img'), may hold values from -0.0859375 to 0.0859375
- ctf: float32 [16, 16384], replicated, may hold values from 0.1 to 1
- ctf_group: int32 [8192], P('img'), may hold values from 0 to 15
- class_id: int32 [6912], P('ref'), may hold values from 0 to 191
- rot_id: int32 [6912], P('ref'), may hold values from 0 to 35
- class_prior: float32 [192], replicated, may hold values from -1 to 1
- rot_prior: float32 [36], replicated, may hold values from -1 to 1
Outputs:
- class_avg: float32 [192, 16384], P('img', 'ref')
- occupancy: float32 [192], replicated
- log_evidence: float32 [8192], P('img')
All inputs are finite; a program needn't handle non-finite values.
Results may differ from a plain program's by a relative error of at most 0.0029.
Values may be sent and summed in bfloat16 or wider, within the bound.
No kernel may reach another device: no remote copies, remote signals or barrier semaphores. Data moves between devices by JAX's collectives and lax.ppermute only.
A program may use at most 128 MiB of HBM per device.

v0:
```python
import jax
import jax.numpy as jnp
from jax import lax
from jax.experimental import pallas as pl
from jax.experimental.pallas import tpu as pltpu
from jax.sharding import Mesh, PartitionSpec as P

NCLASS = 192
NROT = 36
HIGHEST = lax.Precision.HIGHEST
LAST = (((1,), (1,)), ((), ()))
FIRST = (((0,), (0,)), ((), ()))
F32 = jnp.float32
BF16 = jnp.bfloat16


def image_moves(part):
    moves = []
    for x in range(4):
        for h in range(4):
            for y in range(4):
                to_x = (h & 1) * 2 + (y >> 1)
                to_y = y ^ 3 if h >> 1 else y
                moves.append(((x * 4 + h) * 4 + y, (to_x * 4 + (x ^ part)) * 4 + to_y))
    return moves


def flip(step):
    return [(i, i ^ step) for i in range(4)]


def swap_core(block):
    return lax.ppermute(block, "c", [(0, 1), (1, 0)])


def swap_y(block, step):
    return lax.ppermute(block, "y", flip(step))


def split3(value):
    first = lax.reduce_precision(value, 8, 7)
    second = lax.reduce_precision(value - first, 8, 7)
    third = value - first - second
    return first.astype(BF16), second.astype(BF16), third.astype(BF16)


def pick(stacked, index):
    return lax.dynamic_index_in_dim(stacked, index, 0, False)


def hold(values):
    return lax.optimization_barrier(values)


def product_kernel(order, s0, s1, s2a, s2b, s3, blocks, o0, o1, o2, o3):
    outs = (o0, o1, o2, o3)
    half = s2a.shape[0]
    part = half // 2
    for v in range(4):

        @pl.when(order[0] == v)
        def _():
            use = (v, v ^ 1, v ^ 3, v ^ 2)
            for n in range(2):
                rows = pl.ds(n * half, half)
                images = (s0[rows, :], s1[rows, :], (s2a, s2b)[n][...], s3[rows, :])
                score = None
                for d in range(4):
                    term = lax.dot_general(blocks[0, use[d]], images[d], LAST, preferred_element_type=F32)
                    score = term if score is None else score + term
                outs[2 * n][...] = score[:, :part]
                outs[2 * n + 1][...] = score[:, part:]


def product(order, sides, blocks):
    count, _, cols, width = blocks.shape
    part = sides[0].shape[0] // 4
    vmem = pl.BlockSpec(memory_space=pltpu.VMEM)
    return pl.pallas_call(
        product_kernel,
        grid=(count,),
        out_shape=[jax.ShapeDtypeStruct((count * cols, part), F32)] * 4,
        in_specs=[pl.BlockSpec(memory_space=pltpu.SMEM)]
        + [vmem] * 5
        + [pl.BlockSpec((1, 4, cols, width), lambda i: (i, 0, 0, 0))],
        out_specs=[pl.BlockSpec((cols, part), lambda i: (i, 0))] * 4,
        compiler_params=pltpu.CompilerParams(vmem_limit_bytes=40 * 1024 * 1024),
    )(order, *sides, blocks)


def body(images, refs, ctf, ctf_group, class_id, rot_id, class_prior, rot_prior):
    rows, width = images.shape
    cols = refs.shape[0]
    groups = ctf.shape[0]
    quarter, half, mid = rows // 4, rows // 2, width // 2
    a, x, c = lax.axis_index("a"), lax.axis_index("x"), lax.axis_index("c")
    h, y = lax.axis_index("h"), lax.axis_index("y")
    img_place = (a * 4 + x) * 2 + c
    ref_place = h * 4 + y

    gathered = lax.all_gather(refs, ("h", "a", "c"), axis=0).reshape(4, 4, cols, width)
    group_hot = (ctf_group[:, None] == jnp.arange(groups, dtype=jnp.int32)[None, :]).astype(F32)
    ctf_slab = lax.dynamic_slice_in_dim(ctf, ref_place * width, width, 1)
    ctf_rows = jnp.dot(group_hot, ctf_slab, precision=HIGHEST)
    weighted = (ctf_rows * images.astype(F32)).astype(BF16)
    parts = [weighted[p * quarter : (p + 1) * quarter] for p in range(4)]
    moved = [lax.ppermute(parts[p], ("x", "h", "y"), image_moves(p)) for p in range(4)]

    ref_slab = lax.dynamic_slice_in_dim(ctf, img_place * width, width, 1)
    ref_float = refs.astype(F32)
    norm = lax.dot_general(ref_slab * ref_slab, ref_float * ref_float, LAST, precision=HIGHEST)
    norm = norm + swap_core(norm)
    moved, norm = hold((moved, norm))

    s0 = jnp.concatenate([lax.select_n(x ^ h ^ s, *moved) for s in range(4)], 0)
    s1, s3 = swap_y(s0, 1), swap_y(s0, 3)
    norm = norm + lax.ppermute(norm, "x", flip(1))
    norm = norm + lax.ppermute(norm, "x", flip(2))
    s1, s3, norm = hold((s1, s3, norm))
    s2a, s2b = swap_y(s3[:half], 1), swap_y(s1[half:], 3)

    class_match = class_id[:, None] == jnp.arange(NCLASS, dtype=jnp.int32)[None, :]
    rot_match = rot_id[:, None] == jnp.arange(NROT, dtype=jnp.int32)[None, :]
    priors = jnp.sum(jnp.where(class_match, class_prior[None, :], 0.0), axis=1) + jnp.sum(
        jnp.where(rot_match, rot_prior[None, :], 0.0), axis=1
    )
    norm = norm + lax.ppermute(norm, "a", [(0, 1), (1, 0)])
    facts = jnp.concatenate([norm, priors[None], class_id.astype(F32)[None], jnp.zeros((6, cols), F32)])
    near = [facts] + [lax.ppermute(facts, "h", flip(s)) for s in (1, 2, 3)]
    facts = jnp.concatenate([lax.select_n(h ^ t, *near) for t in range(4)], 1)
    own_groups = lax.dynamic_slice_in_dim(ctf_group, (x ^ h) * quarter, quarter, 0)
    own_hot = (own_groups[:, None] == jnp.arange(groups, dtype=jnp.int32)[None, :]).astype(F32)
    offsets = facts[groups][None] - 0.5 * facts[:groups]
    offsets = lax.dot_general(offsets, own_hot, (((0,), (1,)), ((), ())), precision=HIGHEST)
    class_hot = (facts[groups + 1][:, None] == jnp.arange(NCLASS, dtype=F32)[None, :]).astype(BF16)
    s2a, s2b, offsets, class_hot = hold((s2a, s2b, offsets, class_hot))

    turn = (y >> 1) ^ (x & 1)
    order = (2 * turn + ((y & 1) ^ turn)).astype(jnp.int32).reshape(1)
    scores = product(order, (s0, s1, s2a, s2b, s3), gathered)

    def part(s, n):
        return scores[s][n * cols : (n + 1) * cols]

    halves = [
        (lax.ppermute(part(2, n), "x", flip(3)), lax.ppermute(part(2, n + 1), "x", flip(1))) for n in (0, 2)
    ]
    own = []
    for n, (to3, to1) in zip((0, 2), halves):
        part1 = jnp.concatenate([part(1, n) + to3, part(1, n + 1)], 0)
        part3 = jnp.concatenate([part(3, n), part(3, n + 1) + to1], 0)
        here = scores[0][n * cols : (n + 2) * cols] + offsets[n * cols : (n + 2) * cols]
        own.append(here + lax.ppermute(part1, "x", flip(1)) + lax.ppermute(part3, "x", flip(3)))

    own = jnp.concatenate(own, 0)
    top = jnp.max(own, axis=0)
    terms = jnp.concatenate(split3(jnp.exp(own - top[None])), 1)
    class_part = lax.dot_general(class_hot, terms, FIRST, preferred_element_type=F32)
    class_part = class_part[:, :quarter] + class_part[:, quarter : 2 * quarter] + class_part[:, 2 * quarter :]
    payload = jnp.concatenate([class_part, jnp.broadcast_to(top[None], (8, quarter))], axis=0)
    payload = lax.all_to_all(jnp.broadcast_to(payload[None], (4,) + payload.shape), "y", 0, 0, tiled=True)
    tops = payload[:, NCLASS]
    row_top = jnp.max(tops, axis=0)
    mass = jnp.sum(payload[:, :NCLASS] * jnp.exp(tops - row_top[None])[:, None, :], axis=0)
    whole = jnp.sum(mass, axis=0)
    evidence = row_top + jnp.log(whole)
    posterior = mass / whole[None]

    counts_here = jnp.pad(jnp.sum(posterior, axis=1), (0, 2 * quarter - NCLASS))
    sent = jnp.concatenate(
        [
            posterior.astype(BF16),
            jnp.stack(split3(evidence)),
            jnp.concatenate([piece.reshape(2, quarter) for piece in split3(counts_here)]),
            jnp.zeros((7, quarter), BF16),
        ],
        0,
    )
    come = jnp.stack([sent] + [lax.ppermute(sent, "h", flip(s)) for s in (1, 2, 3)])
    come = [pick(come, x ^ h ^ p) for p in range(4)]
    weights = jnp.concatenate([piece[:NCLASS] for piece in come], 1)
    log_evidence = jnp.concatenate([jnp.sum(piece[NCLASS : NCLASS + 3].astype(F32), axis=0) for piece in come])
    counts_part = jnp.zeros((2, quarter), F32)
    for piece in come:
        piece = piece[NCLASS + 3 : NCLASS + 9].astype(F32)
        counts_part = counts_part + (piece[:2] + piece[2:4] + piece[4:])
    counts_part = counts_part.reshape(2 * quarter)

    sums_part = jnp.dot(weights, images, preferred_element_type=F32)
    owned = NCLASS // 16
    count_rows = jnp.pad(jnp.stack(split3(counts_part)), ((0, 1), (0, width - 2 * quarter)))
    outgoing = jnp.concatenate(
        [sums_part.astype(BF16).reshape(16, owned, width), jnp.broadcast_to(count_rows[None], (16, 4, width))], axis=1
    )
    arrived = lax.all_to_all(outgoing, ("a", "x", "c"), 0, 0, tiled=True).astype(F32)
    arrived = jnp.sum(arrived, axis=0)
    counts = jnp.sum(arrived[owned : owned + 3, :NCLASS], axis=0)
    own_counts = lax.dynamic_slice_in_dim(counts, img_place * owned, owned, 0)
    class_avg = arrived[:owned] / (own_counts[:, None] + 1.0)
    occupancy = counts * (NCLASS / (rows * 16))
    return class_avg, occupancy, log_evidence


def solution(mesh):
    split = Mesh(mesh.devices.reshape(2, 4, 2, 4, 4), ("a", "x", "c", "h", "y"))
    img, ref = ("a", "x", "c"), ("h", "y")
    placed = (P(img, ref), P(ref, img), P(), P(img), P(ref), P(ref), P(), P())
    return jax.shard_map(
        body,
        mesh=split,
        in_specs=placed,
        out_specs=(P(img, ref), P(), P(img)),
        check_vma=False,
    )
```

profile of v0, /device:TPU:1, one launch (start us, length us, event | category | flops | bytes accessed | tf_op | source)
XLA Modules:
  0.0 220.6 jit_solution(11866357317999940245)
XLA Ops:
  7.9 2.4 %multiply_convert_fusion = bf16[512,1024]{1,0:T(8,128)(2,1)S(1)} fusion(bf16[512,1024]{1,0:T(8,128)(2,1)} %param.8, s32[512]{0:T(512)} %param.11, f32[16,16384]{1,0:T(8,128)} %param.10, s32[]{:T(128)S(6)} %select_n.253), kind=kOutput, calls=%fused_computation | convolution fusion | flops 102244352 | bytes 2164740 | tf_op jit(solution)/shard_map/dot_general | solution.py:104
  11.1 8.8 %collective-permute-start.1 = (bf16[128,1024]{1,0:T(8,128)(2,1)S(1)}, bf16[128,1024]{1,0:T(8,128)(2,1)S(1)}, u32[]{:S(2)}, u32[]{:S(2)}) collective-permute-start(bf16[128,1024]{1,0:T(8,128)(2,1)S(1)} %get-tuple-element.55), channel_id=1, source_target_pairs={{0,4},{1,5},{2,38},{3,39},{4,68},{5,69},{6,102},{7,103},{8,7},{9,6... | collective-permute-start | bytes 786440 | tf_op jit(solution)/shard_map/ppermute | solution.py:107
  19.9 7.4 %collective-permute-start.2 = (bf16[128,1024]{1,0:T(8,128)(2,1)S(1)}, bf16[128,1024]{1,0:T(8,128)(2,1)S(1)}, u32[]{:S(2)}, u32[]{:S(2)}) collective-permute-start(bf16[128,1024]{1,0:T(8,128)(2,1)S(1)} %get-tuple-element.54), channel_id=1, source_target_pairs={{0,8},{1,9},{2,42},{3,43},{4,72},{5,73},{6,106},{7,107},{8,11},{9,... | collective-permute-start | bytes 786440 | tf_op jit(solution)/shard_map/ppermute | solution.py:107
  27.3 8.2 %collective-permute-start.3 = (bf16[128,1024]{1,0:T(8,128)(2,1)S(1)}, bf16[128,1024]{1,0:T(8,128)(2,1)S(1)}, u32[]{:S(2)}, u32[]{:S(2)}) collective-permute-start(bf16[128,1024]{1,0:T(8,128)(2,1)S(1)} %get-tuple-element.53), channel_id=1, source_target_pairs={{0,12},{1,13},{2,46},{3,47},{4,76},{5,77},{6,110},{7,111},{8,15},{... | collective-permute-start | bytes 786440 | tf_op jit(solution)/shard_map/ppermute | solution.py:107
  40.7 7.5 %collective-permute-done.2 = bf16[128,1024]{1,0:T(8,128)(2,1)S(1)} collective-permute-done((bf16[128,1024]{1,0:T(8,128)(2,1)S(1)}, bf16[128,1024]{1,0:T(8,128)(2,1)S(1)}, u32[]{:S(2)}, u32[]{:S(2)}) %collective-permute-start.2) | collective-permute-done | bytes 262176 | tf_op jit(solution)/shard_map/ppermute | solution.py:107
  48.2 3.4 %collective-permute-done.3 = bf16[128,1024]{1,0:T(8,128)(2,1)S(1)} collective-permute-done((bf16[128,1024]{1,0:T(8,128)(2,1)S(1)}, bf16[128,1024]{1,0:T(8,128)(2,1)S(1)}, u32[]{:S(2)}, u32[]{:S(2)}) %collective-permute-start.3) | collective-permute-done | bytes 262176 | tf_op jit(solution)/shard_map/ppermute | solution.py:107
  51.8 7.5 %collective-permute-start.5 = (bf16[512,1024]{1,0:T(8,128)(2,1)S(1)}, bf16[512,1024]{1,0:T(8,128)(2,1)S(1)}, u32[]{:S(2)}, u32[]{:S(2)}) collective-permute-start(bf16[512,1024]{1,0:T(8,128)(2,1)S(1)} %pad_maximum_fusion.s0), channel_id=1, source_target_pairs={{0,1},{1,0},{2,3},{3,2},{4,5},{5,4},{6,7},{7,6},{8,9},{9,8},{10,11... | collective-permute-start | bytes 3145736 | tf_op jit(solution)/shard_map/ppermute | solution.py:37
  63.4 11.1 %collective-permute-start.8 = (f32[16,432]{1,0:T(8,128)S(1)}, f32[16,432]{1,0:T(8,128)S(1)}, u32[]{:S(2)}, u32[]{:S(2)}) collective-permute-start(f32[16,432]{1,0:T(8,128)S(1)} %add.181), channel_id=1, source_target_pairs={{0,64},{32,96},{64,0},{96,32},{1,65},{33,97},{65,1},{97,33},{2,66}... | collective-permute-start | bytes 82952 | tf_op jit(solution)/shard_map/ppermute | solution.py:118
  75.9 3.9 %collective-permute-done.5.s1 = bf16[512,1024]{1,0:T(8,128)(2,1)S(1)} collective-permute-done((bf16[512,1024]{1,0:T(8,128)(2,1)S(1)}, bf16[512,1024]{1,0:T(8,128)(2,1)S(1)}, u32[]{:S(2)}, u32[]{:S(2)}) %collective-permute-start.5) | collective-permute-done | bytes 1048608 | tf_op jit(solution)/shard_map/ppermute | solution.py:37
  79.8 2.4 %collective-permute-done.6.s3 = bf16[512,1024]{1,0:T(8,128)(2,1)S(1)} collective-permute-done((bf16[512,1024]{1,0:T(8,128)(2,1)S(1)}, bf16[512,1024]{1,0:T(8,128)(2,1)S(1)}, u32[]{:S(2)}, u32[]{:S(2)}) %collective-permute-start.6) | collective-permute-done | bytes 1048608 | tf_op jit(solution)/shard_map/ppermute | solution.py:37
  82.2 12.1 %collective-permute-start.11 = (f32[16,432]{1,0:T(8,128)S(1)}, f32[16,432]{1,0:T(8,128)S(1)}, u32[]{:S(2)}, u32[]{:S(2)}) collective-permute-start(f32[16,432]{1,0:T(8,128)S(1)} %add.182), channel_id=1, source_target_pairs={{0,128},{128,0},{1,129},{129,1},{2,130},{130,2},{3,131},{131,3},{4... | collective-permute-start | bytes 82952 | tf_op jit(solution)/shard_map/ppermute | solution.py:127
  99.0 3.4 %collective-permute-start.14 = (f32[24,432]{1,0:T(8,128)S(1)}, f32[24,432]{1,0:T(8,128)S(1)}, u32[]{:S(2)}, u32[]{:S(2)}) collective-permute-start(f32[24,432]{1,0:T(8,128)S(1)} %maximum_maximum_fusion), channel_id=1, source_target_pairs={{0,12},{4,8},{8,4},{12,0},{1,13},{5,9},{9,5},{13,1},{2,14},{6,10},... | collective-permute-start | bytes 124424 | tf_op jit(solution)/shard_map/ppermute | solution.py:129
  112.0 3.7 %collective-permute-done.10.s2b = bf16[256,1024]{1,0:T(8,128)(2,1)} collective-permute-done((bf16[256,1024]{1,0:T(8,128)(2,1)}, bf16[256,1024]{1,0:T(8,128)(2,1)}, u32[]{:S(2)}, u32[]{:S(2)}) %collective-permute-start.10) | collective-permute-done | bytes 524320 | tf_op jit(solution)/shard_map/ppermute | solution.py:37
  117.2 4.0 %all-gather.3.cloned.1.call-done = bf16[6912,1024]{1,0:T(8,128)(2,1)} async-done(((bf16[432,1024]{1,0:T(8,128)(2,1)}), bf16[6912,1024]{1,0:T(8,128)(2,1)}) %all-gather.3.cloned.1.call-update) | async-done | bytes 14155792 | tf_op jit(solution)/shard_map/all_gather | solution.py:101
  121.2 10.5 %shard_map.103 = (f32[1728,128]{1,0:T(8,128)S(1)}, f32[1728,128]{1,0:T(8,128)S(1)}, f32[1728,128]{1,0:T(8,128)S(1)}, f32[1728,128]{1,0:T(8,128)S(1)}) custom-call(s32[1]{0:T(128)} %bitcast.2.order, bf16[512,1024]{1,0:T(8,128)(2,1)S(1)} %pad_maximum_fusion.s0, bf16[512,1024]{1,0:T(8,128)(2,1)S(1)} %collective-permute-done.5.s1, ...), custom_call_target="tpu_custom_call" | custom-call | tf_op jit(solution)/shard_map/pallas_call | solution.py:79
  131.8 5.1 %collective-permute-start.15 = (f32[432,128]{1,0:T(8,128)S(1)}, f32[432,128]{1,0:T(8,128)S(1)}, u32[]{:S(2)}, u32[]{:S(2)}) collective-permute-start(f32[432,128]{1,0:T(8,128)S(1)} %get-tuple-element.67), channel_id=1, source_target_pairs={{0,96},{32,64},{64,32},{96,0},{1,97},{33,65},{65,33},{97,1},{2,98}... | collective-permute-start | bytes 663560 | tf_op jit(solution)/shard_map/ppermute | solution.py:146
  138.5 4.1 %collective-permute-done.15 = f32[432,128]{1,0:T(8,128)S(1)} collective-permute-done((f32[432,128]{1,0:T(8,128)S(1)}, f32[432,128]{1,0:T(8,128)S(1)}, u32[]{:S(2)}, u32[]{:S(2)}) %collective-permute-start.15) | collective-permute-done | bytes 221216 | tf_op jit(solution)/shard_map/ppermute | solution.py:146
  142.5 4.7 %collective-permute-done.19 = f32[432,128]{1,0:T(8,128)S(1)} collective-permute-done((f32[432,128]{1,0:T(8,128)S(1)}, f32[432,128]{1,0:T(8,128)S(1)}, u32[]{:S(2)}, u32[]{:S(2)}) %collective-permute-start.19) | collective-permute-done | bytes 221216 | tf_op jit(solution)/shard_map/ppermute | solution.py:146
  152.0 6.4 %collective-permute-done.16 = f32[864,128]{1,0:T(8,128)S(1)} collective-permute-done((f32[864,128]{1,0:T(8,128)S(1)}, f32[864,128]{1,0:T(8,128)S(1)}, u32[]{:S(2)}, u32[]{:S(2)}) %collective-permute-start.16) | collective-permute-done | bytes 442400 | tf_op jit(solution)/shard_map/ppermute | solution.py:153
  159.9 8.0 %collective-permute-done.20 = f32[864,128]{1,0:T(8,128)S(1)} collective-permute-done((f32[864,128]{1,0:T(8,128)S(1)}, f32[864,128]{1,0:T(8,128)S(1)}, u32[]{:S(2)}, u32[]{:S(2)}) %collective-permute-start.20) | collective-permute-done | bytes 442400 | tf_op jit(solution)/shard_map/ppermute | solution.py:153
  171.4 10.3 %all_to_all.10 = f32[4,200,128]{2,1,0:T(8,128)S(1)} all-to-all(f32[4,200,128]{2,1,0:T(8,128)S(1)} %broadcast_in_dim.43), channel_id=1, replica_groups=mesh['a'=2,'x'=4,'c'=2,'h'=4,'y'=4] {'y'}, dimensions={0} | all-to-all | bytes 819200 | tf_op jit(solution)/shard_map/all_to_all | solution.py:161
  182.3 3.3 %collective-permute-start.24 = (bf16[208,128]{1,0:T(8,128)(2,1)S(1)}, bf16[208,128]{1,0:T(8,128)(2,1)S(1)}, u32[]{:S(2)}, u32[]{:S(2)}) collective-permute-start(bf16[208,128]{1,0:T(8,128)(2,1)S(1)} %concatenate.52), channel_id=1, source_target_pairs={{0,8},{4,12},{8,0},{12,4},{1,9},{5,13},{9,1},{13,5},{2,10},{6,14},... | collective-permute-start | bytes 159752 | tf_op jit(solution)/shard_map/ppermute | solution.py:179
  192.3 10.1 %all-to-all-start.1 = ((bf16[16,16,1024]{2,1,0:T(8,128)(2,1)}), bf16[16,16,1024]{2,1,0:T(8,128)(2,1)S(1)}, u32[]{:S(2)}, u32[]{:S(2)}) async-start(bf16[16,16,1024]{2,1,0:T(8,128)(2,1)} %pad_maximum_fusion.1), calls=%async_computation.1 | async-start | bytes 1048576 | tf_op jit(solution)/shard_map/all_to_all | solution.py:195
  203.1 9.2 %all-to-all-done.1 = bf16[16,16,1024]{2,1,0:T(8,128)(2,1)S(1)} async-done(((bf16[16,16,1024]{2,1,0:T(8,128)(2,1)}), bf16[16,16,1024]{2,1,0:T(8,128)(2,1)S(1)}, u32[]{:S(2)}, u32[]{:S(2)}) %all-to-all-start.1) | async-done | bytes 524320 | tf_op jit(solution)/shard_map/all_to_all | solution.py:195
  (117 shorter events, 48.5 us)
Async XLA Ops:
  7.2 114.0 %all-gather.3.cloned.1.call-start = ((), (), s32[]{:S(2)}) async-start(), calls=%async_computation.2 | async-start | bytes 15040512 | tf_op jit(solution)/shard_map/all_gather | solution.py:101
  10.4 30.2 %collective-permute-start = (bf16[128,1024]{1,0:T(8,128)(2,1)S(1)}, bf16[128,1024]{1,0:T(8,128)(2,1)S(1)}, u32[]{:S(2)}, u32[]{:S(2)}) collective-permute-start(bf16[128,1024]{1,0:T(8,128)(2,1)S(1)} %get-tuple-element.56), channel_id=1, source_target_pairs={{0,0},{1,1},{2,34},{3,35},{4,64},{5,65},{6,98},{7,99},{8,3},{9,2},... | collective-permute-start | bytes 786440 | tf_op jit(solution)/shard_map/ppermute | solution.py:107
  11.1 29.6 %collective-permute-start.1 = (bf16[128,1024]{1,0:T(8,128)(2,1)S(1)}, bf16[128,1024]{1,0:T(8,128)(2,1)S(1)}, u32[]{:S(2)}, u32[]{:S(2)}) collective-permute-start(bf16[128,1024]{1,0:T(8,128)(2,1)S(1)} %get-tuple-element.55), channel_id=1, source_target_pairs={{0,4},{1,5},{2,38},{3,39},{4,68},{5,69},{6,102},{7,103},{8,7},{9,6... | collective-permute-start | bytes 786440 | tf_op jit(solution)/shard_map/ppermute | solution.py:107
  19.9 28.3 %collective-permute-start.2 = (bf16[128,1024]{1,0:T(8,128)(2,1)S(1)}, bf16[128,1024]{1,0:T(8,128)(2,1)S(1)}, u32[]{:S(2)}, u32[]{:S(2)}) collective-permute-start(bf16[128,1024]{1,0:T(8,128)(2,1)S(1)} %get-tuple-element.54), channel_id=1, source_target_pairs={{0,8},{1,9},{2,42},{3,43},{4,72},{5,73},{6,106},{7,107},{8,11},{9,... | collective-permute-start | bytes 786440 | tf_op jit(solution)/shard_map/ppermute | solution.py:107
  27.3 24.3 %collective-permute-start.3 = (bf16[128,1024]{1,0:T(8,128)(2,1)S(1)}, bf16[128,1024]{1,0:T(8,128)(2,1)S(1)}, u32[]{:S(2)}, u32[]{:S(2)}) collective-permute-start(bf16[128,1024]{1,0:T(8,128)(2,1)S(1)} %get-tuple-element.53), channel_id=1, source_target_pairs={{0,12},{1,13},{2,46},{3,47},{4,76},{5,77},{6,110},{7,111},{8,15},{... | collective-permute-start | bytes 786440 | tf_op jit(solution)/shard_map/ppermute | solution.py:107
  51.8 28.0 %collective-permute-start.5 = (bf16[512,1024]{1,0:T(8,128)(2,1)S(1)}, bf16[512,1024]{1,0:T(8,128)(2,1)S(1)}, u32[]{:S(2)}, u32[]{:S(2)}) collective-permute-start(bf16[512,1024]{1,0:T(8,128)(2,1)S(1)} %pad_maximum_fusion.s0), channel_id=1, source_target_pairs={{0,1},{1,0},{2,3},{3,2},{4,5},{5,4},{6,7},{7,6},{8,9},{9,8},{10,11... | collective-permute-start | bytes 3145736 | tf_op jit(solution)/shard_map/ppermute | solution.py:37
  59.3 22.8 %collective-permute-start.6 = (bf16[512,1024]{1,0:T(8,128)(2,1)S(1)}, bf16[512,1024]{1,0:T(8,128)(2,1)S(1)}, u32[]{:S(2)}, u32[]{:S(2)}) collective-permute-start(bf16[512,1024]{1,0:T(8,128)(2,1)S(1)} %pad_maximum_fusion.s0), channel_id=1, source_target_pairs={{0,3},{1,2},{2,1},{3,0},{4,7},{5,6},{6,5},{7,4},{8,11},{9,10},{10,... | collective-permute-start | bytes 3145736 | tf_op jit(solution)/shard_map/ppermute | solution.py:37
  63.4 12.5 %collective-permute-start.8 = (f32[16,432]{1,0:T(8,128)S(1)}, f32[16,432]{1,0:T(8,128)S(1)}, u32[]{:S(2)}, u32[]{:S(2)}) collective-permute-start(f32[16,432]{1,0:T(8,128)S(1)} %add.181), channel_id=1, source_target_pairs={{0,64},{32,96},{64,0},{96,32},{1,65},{33,97},{65,1},{97,33},{2,66}... | collective-permute-start | bytes 82952 | tf_op jit(solution)/shard_map/ppermute | solution.py:118
  82.2 14.5 %collective-permute-start.11 = (f32[16,432]{1,0:T(8,128)S(1)}, f32[16,432]{1,0:T(8,128)S(1)}, u32[]{:S(2)}, u32[]{:S(2)}) collective-permute-start(f32[16,432]{1,0:T(8,128)S(1)} %add.182), channel_id=1, source_target_pairs={{0,128},{128,0},{1,129},{129,1},{2,130},{130,2},{3,131},{131,3},{4... | collective-permute-start | bytes 82952 | tf_op jit(solution)/shard_map/ppermute | solution.py:127
  96.7 10.5 %collective-permute-start.12 = (f32[24,432]{1,0:T(8,128)S(1)}, f32[24,432]{1,0:T(8,128)S(1)}, u32[]{:S(2)}, u32[]{:S(2)}) collective-permute-start(f32[24,432]{1,0:T(8,128)S(1)} %maximum_maximum_fusion), channel_id=1, source_target_pairs={{0,4},{4,0},{8,12},{12,8},{1,5},{5,1},{9,13},{13,9},{2,6},{6,2},{1... | collective-permute-start | bytes 124424 | tf_op jit(solution)/shard_map/ppermute | solution.py:129
  96.8 10.5 %collective-permute-start.13 = (f32[24,432]{1,0:T(8,128)S(1)}, f32[24,432]{1,0:T(8,128)S(1)}, u32[]{:S(2)}, u32[]{:S(2)}) collective-permute-start(f32[24,432]{1,0:T(8,128)S(1)} %maximum_maximum_fusion), channel_id=1, source_target_pairs={{0,8},{4,12},{8,0},{12,4},{1,9},{5,13},{9,1},{13,5},{2,10},{6,14},... | collective-permute-start | bytes 124424 | tf_op jit(solution)/shard_map/ppermute | solution.py:129
  99.0 9.5 %collective-permute-start.14 = (f32[24,432]{1,0:T(8,128)S(1)}, f32[24,432]{1,0:T(8,128)S(1)}, u32[]{:S(2)}, u32[]{:S(2)}) collective-permute-start(f32[24,432]{1,0:T(8,128)S(1)} %maximum_maximum_fusion), channel_id=1, source_target_pairs={{0,12},{4,8},{8,4},{12,0},{1,13},{5,9},{9,5},{13,1},{2,14},{6,10},... | collective-permute-start | bytes 124424 | tf_op jit(solution)/shard_map/ppermute | solution.py:129
  104.0 11.7 %collective-permute-start.10 = (bf16[256,1024]{1,0:T(8,128)(2,1)}, bf16[256,1024]{1,0:T(8,128)(2,1)}, u32[]{:S(2)}, u32[]{:S(2)}) collective-permute-start(bf16[256,1024]{1,0:T(8,128)(2,1)} %slice.205), channel_id=1, source_target_pairs={{0,3},{1,2},{2,1},{3,0},{4,7},{5,6},{6,5},{7,4},{8,11},{9,10},{10,... | collective-permute-start | bytes 1572872 | tf_op jit(solution)/shard_map/ppermute | solution.py:37
  107.2 10.0 %collective-permute-start.9 = (bf16[256,1024]{1,0:T(8,128)(2,1)}, bf16[256,1024]{1,0:T(8,128)(2,1)}, u32[]{:S(2)}, u32[]{:S(2)}) collective-permute-start(bf16[256,1024]{1,0:T(8,128)(2,1)} %slice.204), channel_id=1, source_target_pairs={{0,1},{1,0},{2,3},{3,2},{4,5},{5,4},{6,7},{7,6},{8,9},{9,8},{10,11... | collective-permute-start | bytes 1572872 | tf_op jit(solution)/shard_map/ppermute | solution.py:37
  131.8 10.8 %collective-permute-start.15 = (f32[432,128]{1,0:T(8,128)S(1)}, f32[432,128]{1,0:T(8,128)S(1)}, u32[]{:S(2)}, u32[]{:S(2)}) collective-permute-start(f32[432,128]{1,0:T(8,128)S(1)} %get-tuple-element.67), channel_id=1, source_target_pairs={{0,96},{32,64},{64,32},{96,0},{1,97},{33,65},{65,33},{97,1},{2,98}... | collective-permute-start | bytes 663560 | tf_op jit(solution)/shard_map/ppermute | solution.py:146
  136.9 10.4 %collective-permute-start.19 = (f32[432,128]{1,0:T(8,128)S(1)}, f32[432,128]{1,0:T(8,128)S(1)}, u32[]{:S(2)}, u32[]{:S(2)}) collective-permute-start(f32[432,128]{1,0:T(8,128)S(1)} %get-tuple-element.64), channel_id=1, source_target_pairs={{0,96},{32,64},{64,32},{96,0},{1,97},{33,65},{65,33},{97,1},{2,98}... | collective-permute-start | bytes 663560 | tf_op jit(solution)/shard_map/ppermute | solution.py:146
  137.0 10.5 %collective-permute-start.17 = (f32[432,128]{1,0:T(8,128)S(1)}, f32[432,128]{1,0:T(8,128)S(1)}, u32[]{:S(2)}, u32[]{:S(2)}) collective-permute-start(f32[432,128]{1,0:T(8,128)S(1)} %get-tuple-element.66), channel_id=1, source_target_pairs={{0,32},{32,0},{64,96},{96,64},{1,33},{33,1},{65,97},{97,65},{2,34}... | collective-permute-start | bytes 663560 | tf_op jit(solution)/shard_map/ppermute | solution.py:146
  137.0 11.2 %collective-permute-start.21 = (f32[432,128]{1,0:T(8,128)S(1)}, f32[432,128]{1,0:T(8,128)S(1)}, u32[]{:S(2)}, u32[]{:S(2)}) collective-permute-start(f32[432,128]{1,0:T(8,128)S(1)} %get-tuple-element.65), channel_id=1, source_target_pairs={{0,32},{32,0},{64,96},{96,64},{1,33},{33,1},{65,97},{97,65},{2,34}... | collective-permute-start | bytes 663560 | tf_op jit(solution)/shard_map/ppermute | solution.py:146
  147.4 11.0 %collective-permute-start.16 = (f32[864,128]{1,0:T(8,128)S(1)}, f32[864,128]{1,0:T(8,128)S(1)}, u32[]{:S(2)}, u32[]{:S(2)}) collective-permute-start(f32[864,128]{1,0:T(8,128)S(1)} %pad_maximum_fusion.2), channel_id=1, source_target_pairs={{0,32},{32,0},{64,96},{96,64},{1,33},{33,1},{65,97},{97,65},{2,34}... | collective-permute-start | bytes 1327112 | tf_op jit(solution)/shard_map/ppermute | solution.py:153
  148.3 11.6 %collective-permute-start.18 = (f32[864,128]{1,0:T(8,128)S(1)}, f32[864,128]{1,0:T(8,128)S(1)}, u32[]{:S(2)}, u32[]{:S(2)}) collective-permute-start(f32[864,128]{1,0:T(8,128)S(1)} %pad_maximum_fusion.3), channel_id=1, source_target_pairs={{0,96},{32,64},{64,32},{96,0},{1,97},{33,65},{65,33},{97,1},{2,98}... | collective-permute-start | bytes 1327112 | tf_op jit(solution)/shard_map/ppermute | solution.py:153
  150.7 17.2 %collective-permute-start.20 = (f32[864,128]{1,0:T(8,128)S(1)}, f32[864,128]{1,0:T(8,128)S(1)}, u32[]{:S(2)}, u32[]{:S(2)}) collective-permute-start(f32[864,128]{1,0:T(8,128)S(1)} %pad_maximum_fusion.4), channel_id=1, source_target_pairs={{0,32},{32,0},{64,96},{96,64},{1,33},{33,1},{65,97},{97,65},{2,34}... | collective-permute-start | bytes 1327112 | tf_op jit(solution)/shard_map/ppermute | solution.py:153
  151.1 18.3 %collective-permute-start.22 = (f32[864,128]{1,0:T(8,128)S(1)}, f32[864,128]{1,0:T(8,128)S(1)}, u32[]{:S(2)}, u32[]{:S(2)}) collective-permute-start(f32[864,128]{1,0:T(8,128)S(1)} %pad_maximum_fusion.5), channel_id=1, source_target_pairs={{0,96},{32,64},{64,32},{96,0},{1,97},{33,65},{65,33},{97,1},{2,98}... | collective-permute-start | bytes 1327112 | tf_op jit(solution)/shard_map/ppermute | solution.py:153
  182.3 7.0 %collective-permute-start.24 = (bf16[208,128]{1,0:T(8,128)(2,1)S(1)}, bf16[208,128]{1,0:T(8,128)(2,1)S(1)}, u32[]{:S(2)}, u32[]{:S(2)}) collective-permute-start(bf16[208,128]{1,0:T(8,128)(2,1)S(1)} %concatenate.52), channel_id=1, source_target_pairs={{0,8},{4,12},{8,0},{12,4},{1,9},{5,13},{9,1},{13,5},{2,10},{6,14},... | collective-permute-start | bytes 159752 | tf_op jit(solution)/shard_map/ppermute | solution.py:179
  192.3 19.9 %all-to-all-start.1 = ((bf16[16,16,1024]{2,1,0:T(8,128)(2,1)}), bf16[16,16,1024]{2,1,0:T(8,128)(2,1)S(1)}, u32[]{:S(2)}, u32[]{:S(2)}) async-start(bf16[16,16,1024]{2,1,0:T(8,128)(2,1)} %pad_maximum_fusion.1), calls=%async_computation.1 | async-start | bytes 1048576 | tf_op jit(solution)/shard_map/all_to_all | solution.py:195
  (12 other events, 262.3 us)
Sparse Core Ops, SparseCore 0:
  9.8 111.2 all-gather.2
where the time goes:
time: 221 us
  starting transfers between devices  94.4 us (43%)
  waiting for transfers between devices  73.1 us (33%)
  between operations  14.5 us (7%)
  Pallas kernels  10.5 us (5%)
  blocking collectives  10.3 us (5%)
  matrix products  7.59 us (3%)
  other arithmetic  6.19 us (3%)
  local copies, waits for them, and re-layouts  4 us (2%)
    ppermute x4, starting transfers between devices, body(): lax.ppermute(parts[p], ('x', 'h', 'y'), image_moves(p))  25 us
    ppermute x2, waiting for transfers between devices, body(): lax.ppermute(part1, 'x', flip(1))  14.5 us
    ppermute x1, starting transfers between devices, body(): norm = norm + lax.ppermute(norm, 'a', [(0, 1), (1, 0)])  12.1 us
    ppermute x4, waiting for transfers between devices, swap_y(): return lax.ppermute(block, 'y', flip(step))  11.4 us
    ppermute x1, starting transfers between devices, body(): norm = norm + lax.ppermute(norm, 'x', flip(2))  11.1 us
    ppermute x4, waiting for transfers between devices, body(): lax.ppermute(parts[p], ('x', 'h', 'y'), image_moves(p))  10.9 us
    pallas_call x1, Pallas kernels, product(): pl.pallas_call(product_kernel, grid=(count,), out_shape=[jax.ShapeDtypeSt...  10.5 us
    all_to_all x1, blocking collectives, body(): lax.all_to_all(jnp.broadcast_to(payload[None], (4,) + payload.shape), 'y'...  10.3 us
  transfers between devices with their start and end apart: 28, of which 22 were waited for; matrix products, arithmetic and copies ran while one was open for 6% of the time, Pallas kernels for 0%

commit v1 on v0

--- a/solution.py
+++ b/solution.py
@@ -137,19 +137,15 @@
 
     turn = (y >> 1) ^ (x & 1)
     order = (2 * turn + ((y & 1) ^ turn)).astype(jnp.int32).reshape(1)
-    scores = product(order, (s0, s1, s2a, s2b, s3), gathered)
-
-    def part(s, n):
-        return scores[s][n * cols : (n + 1) * cols]
-
-    halves = [
-        (lax.ppermute(part(2, n), "x", flip(3)), lax.ppermute(part(2, n + 1), "x", flip(1))) for n in (0, 2)
-    ]
     own = []
-    for n, (to3, to1) in zip((0, 2), halves):
-        part1 = jnp.concatenate([part(1, n) + to3, part(1, n + 1)], 0)
-        part3 = jnp.concatenate([part(3, n), part(3, n + 1) + to1], 0)
-        here = scores[0][n * cols : (n + 2) * cols] + offsets[n * cols : (n + 2) * cols]
+    products = product(order, (s0, s1, s2a, s2b, s3), gathered)
+    for n in (0, 2):
+        scores = [piece[n * cols : (n + 2) * cols] for piece in products]
+        to3 = lax.ppermute(scores[2][:cols], "x", flip(3))
+        to1 = lax.ppermute(scores[2][cols:], "x", flip(1))
+        part1 = jnp.concatenate([scores[1][:cols] + to3, scores[1][cols:]], 0)
+        part3 = jnp.concatenate([scores[3][:cols], scores[3][cols:] + to1], 0)
+        here = scores[0] + offsets[n * cols : (n + 2) * cols]
         own.append(here + lax.ppermute(part1, "x", flip(1)) + lax.ppermute(part3, "x", flip(3)))
 
     own = jnp.concatenate(own, 0)
@@ -186,15 +182,20 @@
         counts_part = counts_part + (piece[:2] + piece[2:4] + piece[4:])
     counts_part = counts_part.reshape(2 * quarter)
 
-    sums_part = jnp.dot(weights, images, preferred_element_type=F32)
     owned = NCLASS // 16
-    count_rows = jnp.pad(jnp.stack(split3(counts_part)), ((0, 1), (0, width - 2 * quarter)))
-    outgoing = jnp.concatenate(
-        [sums_part.astype(BF16).reshape(16, owned, width), jnp.broadcast_to(count_rows[None], (16, 4, width))], axis=1
-    )
-    arrived = lax.all_to_all(outgoing, ("a", "x", "c"), 0, 0, tiled=True).astype(F32)
-    arrived = jnp.sum(arrived, axis=0)
-    counts = jnp.sum(arrived[owned : owned + 3, :NCLASS], axis=0)
+    weights = weights.reshape(8, 2, owned, rows)
+    count_row = jnp.pad(counts_part, (0, width - 2 * quarter))
+
+    def sums_of(core):
+        kept = jnp.pad(lax.dynamic_index_in_dim(weights, core, 1, False), ((0, 0), (0, 4), (0, 0)))
+        sums = jnp.dot(kept.reshape(8 * (owned + 4), rows), images, preferred_element_type=F32)
+        sums = sums.reshape(8, owned + 4, width)
+        place = lax.broadcasted_iota(jnp.int32, sums.shape, 1)
+        return jnp.where(place == owned, count_row[None, None], sums)
+
+    outgoing = sums_of(c) + swap_core(sums_of(1 - c))
+    arrived = jnp.sum(lax.all_to_all(outgoing, ("a", "x"), 0, 0, tiled=True), axis=0)
+    counts = arrived[owned, :NCLASS]
     own_counts = lax.dynamic_slice_in_dim(counts, img_place * owned, owned, 0)
     class_avg = arrived[:owned] / (own_counts[:, None] + 1.0)
     occupancy = counts * (NCLASS / (rows * 16))

time: 221 us -> 221 us (level)
    all_to_all x1, starting transfers between devices: 10.1 us -> 4 us  [body(): lax.all_to_all(outgoing, ('a', 'x'), 0, 0, tiled=True)]
    ppermute x1 -> x2, starting transfers between devices: 1.88 us -> 7.81 us  [swap_core(): return lax.ppermute(block, 'c', [(0, 1), (1, 0)])]
  transfers between devices with their start and end apart: 28 -> 29, of which waited for: 22 -> 23; matrix products, arithmetic and copies ran while one was open for 6% -> 6% of each run, Pallas kernels for 0% -> 0%
where the time goes in v1:
time: 221 us; the launch traced here: 220 us
  starting transfers between devices  94.2 us (43%)
  waiting for transfers between devices  73 us (33%)
  between operations  14.5 us (7%)
  Pallas kernels  10.5 us (5%)
  blocking collectives  10.3 us (5%)
  matrix products  8.61 us (4%)
  other arithmetic  5.18 us (2%)
  local copies, waits for them, and re-layouts  4.06 us (2%)
    ppermute x4, starting transfers between devices, body(): lax.ppermute(parts[p], ('x', 'h', 'y'), image_moves(p))  25 us
    ppermute x2, waiting for transfers between devices, body(): lax.ppermute(part1, 'x', flip(1))  14.5 us
    ppermute x1, starting transfers between devices, body(): norm = norm + lax.ppermute(norm, 'a', [(0, 1), (1, 0)])  12.1 us
    ppermute x4, waiting for transfers between devices, swap_y(): return lax.ppermute(block, 'y', flip(step))  11.5 us
    ppermute x1, starting transfers between devices, body(): norm = norm + lax.ppermute(norm, 'x', flip(2))  11.1 us
    ppermute x4, waiting for transfers between devices, body(): lax.ppermute(parts[p], ('x', 'h', 'y'), image_moves(p))  10.9 us
    pallas_call x1, Pallas kernels, product(): pl.pallas_call(product_kernel, grid=(count,), out_shape=[jax.ShapeDtypeSt...  10.5 us
    all_to_all x1, blocking collectives, body(): lax.all_to_all(jnp.broadcast_to(payload[None], (4,) + payload.shape), 'y'...  10.3 us
  transfers between devices with their start and end apart: 29, of which 23 were waited for; matrix products, arithmetic and copies ran while one was open for 6% of the time, Pallas kernels for 0%

profile of v1, /device:TPU:1, one launch (start us, length us, event | category | flops | bytes accessed | tf_op | source)
XLA Modules:
  0.0 220.4 jit_solution(17504702433320085938)
XLA Ops:
  7.9 2.4 %multiply_convert_fusion = bf16[512,1024]{1,0:T(8,128)(2,1)S(1)} fusion(bf16[512,1024]{1,0:T(8,128)(2,1)} %param.8, s32[512]{0:T(512)} %param.11, f32[16,16384]{1,0:T(8,128)} %param.10, s32[]{:T(128)S(6)} %select_n.267), kind=kOutput, calls=%fused_computation | convolution fusion | flops 102244352 | bytes 2164740 | tf_op jit(solution)/shard_map/dot_general | solution.py:104
  11.1 8.8 %collective-permute-start.1 = (bf16[128,1024]{1,0:T(8,128)(2,1)S(1)}, bf16[128,1024]{1,0:T(8,128)(2,1)S(1)}, u32[]{:S(2)}, u32[]{:S(2)}) collective-permute-start(bf16[128,1024]{1,0:T(8,128)(2,1)S(1)} %get-tuple-element.55), channel_id=1, source_target_pairs={{0,4},{1,5},{2,38},{3,39},{4,68},{5,69},{6,102},{7,103},{8,7},{9,6... | collective-permute-start | bytes 786440 | tf_op jit(solution)/shard_map/ppermute | solution.py:107
  19.9 7.4 %collective-permute-start.2 = (bf16[128,1024]{1,0:T(8,128)(2,1)S(1)}, bf16[128,1024]{1,0:T(8,128)(2,1)S(1)}, u32[]{:S(2)}, u32[]{:S(2)}) collective-permute-start(bf16[128,1024]{1,0:T(8,128)(2,1)S(1)} %get-tuple-element.54), channel_id=1, source_target_pairs={{0,8},{1,9},{2,42},{3,43},{4,72},{5,73},{6,106},{7,107},{8,11},{9,... | collective-permute-start | bytes 786440 | tf_op jit(solution)/shard_map/ppermute | solution.py:107
  27.3 8.2 %collective-permute-start.3 = (bf16[128,1024]{1,0:T(8,128)(2,1)S(1)}, bf16[128,1024]{1,0:T(8,128)(2,1)S(1)}, u32[]{:S(2)}, u32[]{:S(2)}) collective-permute-start(bf16[128,1024]{1,0:T(8,128)(2,1)S(1)} %get-tuple-element.53), channel_id=1, source_target_pairs={{0,12},{1,13},{2,46},{3,47},{4,76},{5,77},{6,110},{7,111},{8,15},{... | collective-permute-start | bytes 786440 | tf_op jit(solution)/shard_map/ppermute | solution.py:107
  40.7 7.5 %collective-permute-done.2 = bf16[128,1024]{1,0:T(8,128)(2,1)S(1)} collective-permute-done((bf16[128,1024]{1,0:T(8,128)(2,1)S(1)}, bf16[128,1024]{1,0:T(8,128)(2,1)S(1)}, u32[]{:S(2)}, u32[]{:S(2)}) %collective-permute-start.2) | collective-permute-done | bytes 262176 | tf_op jit(solution)/shard_map/ppermute | solution.py:107
  48.2 3.4 %collective-permute-done.3 = bf16[128,1024]{1,0:T(8,128)(2,1)S(1)} collective-permute-done((bf16[128,1024]{1,0:T(8,128)(2,1)S(1)}, bf16[128,1024]{1,0:T(8,128)(2,1)S(1)}, u32[]{:S(2)}, u32[]{:S(2)}) %collective-permute-start.3) | collective-permute-done | bytes 262176 | tf_op jit(solution)/shard_map/ppermute | solution.py:107
  51.8 7.5 %collective-permute-start.5 = (bf16[512,1024]{1,0:T(8,128)(2,1)S(1)}, bf16[512,1024]{1,0:T(8,128)(2,1)S(1)}, u32[]{:S(2)}, u32[]{:S(2)}) collective-permute-start(bf16[512,1024]{1,0:T(8,128)(2,1)S(1)} %pad_maximum_fusion.s0), channel_id=1, source_target_pairs={{0,1},{1,0},{2,3},{3,2},{4,5},{5,4},{6,7},{7,6},{8,9},{9,8},{10,11... | collective-permute-start | bytes 3145736 | tf_op jit(solution)/shard_map/ppermute | solution.py:37
  63.4 11.1 %collective-permute-start.8 = (f32[16,432]{1,0:T(8,128)S(1)}, f32[16,432]{1,0:T(8,128)S(1)}, u32[]{:S(2)}, u32[]{:S(2)}) collective-permute-start(f32[16,432]{1,0:T(8,128)S(1)} %add.203), channel_id=1, source_target_pairs={{0,64},{32,96},{64,0},{96,32},{1,65},{33,97},{65,1},{97,33},{2,66}... | collective-permute-start | bytes 82952 | tf_op jit(solution)/shard_map/ppermute | solution.py:118
  75.9 3.9 %collective-permute-done.5.s1 = bf16[512,1024]{1,0:T(8,128)(2,1)S(1)} collective-permute-done((bf16[512,1024]{1,0:T(8,128)(2,1)S(1)}, bf16[512,1024]{1,0:T(8,128)(2,1)S(1)}, u32[]{:S(2)}, u32[]{:S(2)}) %collective-permute-start.5) | collective-permute-done | bytes 1048608 | tf_op jit(solution)/shard_map/ppermute | solution.py:37
  82.2 12.1 %collective-permute-start.11 = (f32[16,432]{1,0:T(8,128)S(1)}, f32[16,432]{1,0:T(8,128)S(1)}, u32[]{:S(2)}, u32[]{:S(2)}) collective-permute-start(f32[16,432]{1,0:T(8,128)S(1)} %add.204), channel_id=1, source_target_pairs={{0,128},{128,0},{1,129},{129,1},{2,130},{130,2},{3,131},{131,3},{4... | collective-permute-start | bytes 82952 | tf_op jit(solution)/shard_map/ppermute | solution.py:127
  99.0 3.4 %collective-permute-start.14 = (f32[24,432]{1,0:T(8,128)S(1)}, f32[24,432]{1,0:T(8,128)S(1)}, u32[]{:S(2)}, u32[]{:S(2)}) collective-permute-start(f32[24,432]{1,0:T(8,128)S(1)} %maximum_maximum_fusion), channel_id=1, source_target_pairs={{0,12},{4,8},{8,4},{12,0},{1,13},{5,9},{9,5},{13,1},{2,14},{6,10},... | collective-permute-start | bytes 124424 | tf_op jit(solution)/shard_map/ppermute | solution.py:129
  112.0 3.7 %collective-permute-done.10.s2b = bf16[256,1024]{1,0:T(8,128)(2,1)} collective-permute-done((bf16[256,1024]{1,0:T(8,128)(2,1)}, bf16[256,1024]{1,0:T(8,128)(2,1)}, u32[]{:S(2)}, u32[]{:S(2)}) %collective-permute-start.10) | collective-permute-done | bytes 524320 | tf_op jit(solution)/shard_map/ppermute | solution.py:37
  117.2 4.0 %all-gather.3.cloned.1.call-done = bf16[6912,1024]{1,0:T(8,128)(2,1)} async-done(((bf16[432,1024]{1,0:T(8,128)(2,1)}), bf16[6912,1024]{1,0:T(8,128)(2,1)}) %all-gather.3.cloned.1.call-update) | async-done | bytes 14155792 | tf_op jit(solution)/shard_map/all_gather | solution.py:101
  121.2 10.5 %shard_map.103 = (f32[1728,128]{1,0:T(8,128)S(1)}, f32[1728,128]{1,0:T(8,128)S(1)}, f32[1728,128]{1,0:T(8,128)S(1)}, f32[1728,128]{1,0:T(8,128)S(1)}) custom-call(s32[1]{0:T(128)} %bitcast.2.order, bf16[512,1024]{1,0:T(8,128)(2,1)S(1)} %pad_maximum_fusion.s0, bf16[512,1024]{1,0:T(8,128)(2,1)S(1)} %collective-permute-done.5.s1, ...), custom_call_target="tpu_custom_call" | custom-call | tf_op jit(solution)/shard_map/pallas_call | solution.py:79
  131.8 5.1 %collective-permute-start.15 = (f32[432,128]{1,0:T(8,128)S(1)}, f32[432,128]{1,0:T(8,128)S(1)}, u32[]{:S(2)}, u32[]{:S(2)}) collective-permute-start(f32[432,128]{1,0:T(8,128)S(1)} %get-tuple-element.67), channel_id=1, source_target_pairs={{0,96},{32,64},{64,32},{96,0},{1,97},{33,65},{65,33},{97,1},{2,98}... | collective-permute-start | bytes 663560 | tf_op jit(solution)/shard_map/ppermute | solution.py:144
  138.5 4.1 %collective-permute-done.15 = f32[432,128]{1,0:T(8,128)S(1)} collective-permute-done((f32[432,128]{1,0:T(8,128)S(1)}, f32[432,128]{1,0:T(8,128)S(1)}, u32[]{:S(2)}, u32[]{:S(2)}) %collective-permute-start.15) | collective-permute-done | bytes 221216 | tf_op jit(solution)/shard_map/ppermute | solution.py:144
  142.5 4.7 %collective-permute-done.19 = f32[432,128]{1,0:T(8,128)S(1)} collective-permute-done((f32[432,128]{1,0:T(8,128)S(1)}, f32[432,128]{1,0:T(8,128)S(1)}, u32[]{:S(2)}, u32[]{:S(2)}) %collective-permute-start.19) | collective-permute-done | bytes 221216 | tf_op jit(solution)/shard_map/ppermute | solution.py:144
  152.0 6.4 %collective-permute-done.16 = f32[864,128]{1,0:T(8,128)S(1)} collective-permute-done((f32[864,128]{1,0:T(8,128)S(1)}, f32[864,128]{1,0:T(8,128)S(1)}, u32[]{:S(2)}, u32[]{:S(2)}) %collective-permute-start.16) | collective-permute-done | bytes 442400 | tf_op jit(solution)/shard_map/ppermute | solution.py:149
  159.9 8.0 %collective-permute-done.20 = f32[864,128]{1,0:T(8,128)S(1)} collective-permute-done((f32[864,128]{1,0:T(8,128)S(1)}, f32[864,128]{1,0:T(8,128)S(1)}, u32[]{:S(2)}, u32[]{:S(2)}) %collective-permute-start.20) | collective-permute-done | bytes 442400 | tf_op jit(solution)/shard_map/ppermute | solution.py:149
  171.4 10.3 %all_to_all.10 = f32[4,200,128]{2,1,0:T(8,128)S(1)} all-to-all(f32[4,200,128]{2,1,0:T(8,128)S(1)} %broadcast_in_dim.82), channel_id=1, replica_groups=mesh['a'=2,'x'=4,'c'=2,'h'=4,'y'=4] {'y'}, dimensions={0} | all-to-all | bytes 819200 | tf_op jit(solution)/shard_map/all_to_all | solution.py:157
  182.3 3.3 %collective-permute-start.24 = (bf16[208,128]{1,0:T(8,128)(2,1)S(1)}, bf16[208,128]{1,0:T(8,128)(2,1)S(1)}, u32[]{:S(2)}, u32[]{:S(2)}) collective-permute-start(bf16[208,128]{1,0:T(8,128)(2,1)S(1)} %concatenate.58), channel_id=1, source_target_pairs={{0,8},{4,12},{8,0},{12,4},{1,9},{5,13},{9,1},{13,5},{2,10},{6,14},... | collective-permute-start | bytes 159752 | tf_op jit(solution)/shard_map/ppermute | solution.py:175
  191.4 5.9 %collective-permute-start.26 = (f32[8,16,1024]{2,1,0:T(8,128)S(1)}, f32[8,16,1024]{2,1,0:T(8,128)S(1)}, u32[]{:S(2)}, u32[]{:S(2)}) collective-permute-start(f32[8,16,1024]{2,1,0:T(8,128)S(1)} %convolution_select_fusion), channel_id=1, source_target_pairs={{0,16},{16,0},{1,17},{17,1},{2,18},{18,2},{3,19},{19,3},{4,20},{20... | collective-permute-start | bytes 1572872 | tf_op jit(solution)/shard_map/ppermute | solution.py:33
  200.0 4.0 %all-to-all-start.1 = ((f32[8,16,1024]{2,1,0:T(8,128)}), f32[8,16,1024]{2,1,0:T(8,128)S(1)}, u32[]{:S(2)}, u32[]{:S(2)}) async-start(f32[8,16,1024]{2,1,0:T(8,128)} %fusion.10), calls=%async_computation.1 | async-start | bytes 1048576 | tf_op jit(solution)/shard_map/all_to_all | solution.py:197
  204.6 7.6 %all-to-all-done.1 = f32[8,16,1024]{2,1,0:T(8,128)S(1)} async-done(((f32[8,16,1024]{2,1,0:T(8,128)}), f32[8,16,1024]{2,1,0:T(8,128)S(1)}, u32[]{:S(2)}, u32[]{:S(2)}) %all-to-all-start.1) | async-done | bytes 524320 | tf_op jit(solution)/shard_map/all_to_all | solution.py:197
  (125 shorter events, 52.5 us)
Async XLA Ops:
  7.2 114.0 %all-gather.3.cloned.1.call-start = ((), (), s32[]{:S(2)}) async-start(), calls=%async_computation.2 | async-start | bytes 15040512 | tf_op jit(solution)/shard_map/all_gather | solution.py:101
  10.4 30.2 %collective-permute-start = (bf16[128,1024]{1,0:T(8,128)(2,1)S(1)}, bf16[128,1024]{1,0:T(8,128)(2,1)S(1)}, u32[]{:S(2)}, u32[]{:S(2)}) collective-permute-start(bf16[128,1024]{1,0:T(8,128)(2,1)S(1)} %get-tuple-element.56), channel_id=1, source_target_pairs={{0,0},{1,1},{2,34},{3,35},{4,64},{5,65},{6,98},{7,99},{8,3},{9,2},... | collective-permute-start | bytes 786440 | tf_op jit(solution)/shard_map/ppermute | solution.py:107
  11.1 29.6 %collective-permute-start.1 = (bf16[128,1024]{1,0:T(8,128)(2,1)S(1)}, bf16[128,1024]{1,0:T(8,128)(2,1)S(1)}, u32[]{:S(2)}, u32[]{:S(2)}) collective-permute-start(bf16[128,1024]{1,0:T(8,128)(2,1)S(1)} %get-tuple-element.55), channel_id=1, source_target_pairs={{0,4},{1,5},{2,38},{3,39},{4,68},{5,69},{6,102},{7,103},{8,7},{9,6... | collective-permute-start | bytes 786440 | tf_op jit(solution)/shard_map/ppermute | solution.py:107
  19.9 28.3 %collective-permute-start.2 = (bf16[128,1024]{1,0:T(8,128)(2,1)S(1)}, bf16[128,1024]{1,0:T(8,128)(2,1)S(1)}, u32[]{:S(2)}, u32[]{:S(2)}) collective-permute-start(bf16[128,1024]{1,0:T(8,128)(2,1)S(1)} %get-tuple-element.54), channel_id=1, source_target_pairs={{0,8},{1,9},{2,42},{3,43},{4,72},{5,73},{6,106},{7,107},{8,11},{9,... | collective-permute-start | bytes 786440 | tf_op jit(solution)/shard_map/ppermute | solution.py:107
  27.3 24.3 %collective-permute-start.3 = (bf16[128,1024]{1,0:T(8,128)(2,1)S(1)}, bf16[128,1024]{1,0:T(8,128)(2,1)S(1)}, u32[]{:S(2)}, u32[]{:S(2)}) collective-permute-start(bf16[128,1024]{1,0:T(8,128)(2,1)S(1)} %get-tuple-element.53), channel_id=1, source_target_pairs={{0,12},{1,13},{2,46},{3,47},{4,76},{5,77},{6,110},{7,111},{8,15},{... | collective-permute-start | bytes 786440 | tf_op jit(solution)/shard_map/ppermute | solution.py:107
  51.8 28.0 %collective-permute-start.5 = (bf16[512,1024]{1,0:T(8,128)(2,1)S(1)}, bf16[512,1024]{1,0:T(8,128)(2,1)S(1)}, u32[]{:S(2)}, u32[]{:S(2)}) collective-permute-start(bf16[512,1024]{1,0:T(8,128)(2,1)S(1)} %pad_maximum_fusion.s0), channel_id=1, source_target_pairs={{0,1},{1,0},{2,3},{3,2},{4,5},{5,4},{6,7},{7,6},{8,9},{9,8},{10,11... | collective-permute-start | bytes 3145736 | tf_op jit(solution)/shard_map/ppermute | solution.py:37
  59.3 22.8 %collective-permute-start.6 = (bf16[512,1024]{1,0:T(8,128)(2,1)S(1)}, bf16[512,1024]{1,0:T(8,128)(2,1)S(1)}, u32[]{:S(2)}, u32[]{:S(2)}) collective-permute-start(bf16[512,1024]{1,0:T(8,128)(2,1)S(1)} %pad_maximum_fusion.s0), channel_id=1, source_target_pairs={{0,3},{1,2},{2,1},{3,0},{4,7},{5,6},{6,5},{7,4},{8,11},{9,10},{10,... | collective-permute-start | bytes 3145736 | tf_op jit(solution)/shard_map/ppermute | solution.py:37
  63.4 12.5 %collective-permute-start.8 = (f32[16,432]{1,0:T(8,128)S(1)}, f32[16,432]{1,0:T(8,128)S(1)}, u32[]{:S(2)}, u32[]{:S(2)}) collective-permute-start(f32[16,432]{1,0:T(8,128)S(1)} %add.203), channel_id=1, source_target_pairs={{0,64},{32,96},{64,0},{96,32},{1,65},{33,97},{65,1},{97,33},{2,66}... | collective-permute-start | bytes 82952 | tf_op jit(solution)/shard_map/ppermute | solution.py:118
  82.2 14.5 %collective-permute-start.11 = (f32[16,432]{1,0:T(8,128)S(1)}, f32[16,432]{1,0:T(8,128)S(1)}, u32[]{:S(2)}, u32[]{:S(2)}) collective-permute-start(f32[16,432]{1,0:T(8,128)S(1)} %add.204), channel_id=1, source_target_pairs={{0,128},{128,0},{1,129},{129,1},{2,130},{130,2},{3,131},{131,3},{4... | collective-permute-start | bytes 82952 | tf_op jit(solution)/shard_map/ppermute | solution.py:127
  96.7 10.5 %collective-permute-start.12 = (f32[24,432]{1,0:T(8,128)S(1)}, f32[24,432]{1,0:T(8,128)S(1)}, u32[]{:S(2)}, u32[]{:S(2)}) collective-permute-start(f32[24,432]{1,0:T(8,128)S(1)} %maximum_maximum_fusion), channel_id=1, source_target_pairs={{0,4},{4,0},{8,12},{12,8},{1,5},{5,1},{9,13},{13,9},{2,6},{6,2},{1... | collective-permute-start | bytes 124424 | tf_op jit(solution)/shard_map/ppermute | solution.py:129
  96.8 10.5 %collective-permute-start.13 = (f32[24,432]{1,0:T(8,128)S(1)}, f32[24,432]{1,0:T(8,128)S(1)}, u32[]{:S(2)}, u32[]{:S(2)}) collective-permute-start(f32[24,432]{1,0:T(8,128)S(1)} %maximum_maximum_fusion), channel_id=1, source_target_pairs={{0,8},{4,12},{8,0},{12,4},{1,9},{5,13},{9,1},{13,5},{2,10},{6,14},... | collective-permute-start | bytes 124424 | tf_op jit(solution)/shard_map/ppermute | solution.py:129
  99.0 9.5 %collective-permute-start.14 = (f32[24,432]{1,0:T(8,128)S(1)}, f32[24,432]{1,0:T(8,128)S(1)}, u32[]{:S(2)}, u32[]{:S(2)}) collective-permute-start(f32[24,432]{1,0:T(8,128)S(1)} %maximum_maximum_fusion), channel_id=1, source_target_pairs={{0,12},{4,8},{8,4},{12,0},{1,13},{5,9},{9,5},{13,1},{2,14},{6,10},... | collective-permute-start | bytes 124424 | tf_op jit(solution)/shard_map/ppermute | solution.py:129
  104.0 11.7 %collective-permute-start.10 = (bf16[256,1024]{1,0:T(8,128)(2,1)}, bf16[256,1024]{1,0:T(8,128)(2,1)}, u32[]{:S(2)}, u32[]{:S(2)}) collective-permute-start(bf16[256,1024]{1,0:T(8,128)(2,1)} %slice.215), channel_id=1, source_target_pairs={{0,3},{1,2},{2,1},{3,0},{4,7},{5,6},{6,5},{7,4},{8,11},{9,10},{10,... | collective-permute-start | bytes 1572872 | tf_op jit(solution)/shard_map/ppermute | solution.py:37
  107.2 10.0 %collective-permute-start.9 = (bf16[256,1024]{1,0:T(8,128)(2,1)}, bf16[256,1024]{1,0:T(8,128)(2,1)}, u32[]{:S(2)}, u32[]{:S(2)}) collective-permute-start(bf16[256,1024]{1,0:T(8,128)(2,1)} %slice.214), channel_id=1, source_target_pairs={{0,1},{1,0},{2,3},{3,2},{4,5},{5,4},{6,7},{7,6},{8,9},{9,8},{10,11... | collective-permute-start | bytes 1572872 | tf_op jit(solution)/shard_map/ppermute | solution.py:37
  131.8 10.8 %collective-permute-start.15 = (f32[432,128]{1,0:T(8,128)S(1)}, f32[432,128]{1,0:T(8,128)S(1)}, u32[]{:S(2)}, u32[]{:S(2)}) collective-permute-start(f32[432,128]{1,0:T(8,128)S(1)} %get-tuple-element.67), channel_id=1, source_target_pairs={{0,96},{32,64},{64,32},{96,0},{1,97},{33,65},{65,33},{97,1},{2,98}... | collective-permute-start | bytes 663560 | tf_op jit(solution)/shard_map/ppermute | solution.py:144
  136.9 10.4 %collective-permute-start.19 = (f32[432,128]{1,0:T(8,128)S(1)}, f32[432,128]{1,0:T(8,128)S(1)}, u32[]{:S(2)}, u32[]{:S(2)}) collective-permute-start(f32[432,128]{1,0:T(8,128)S(1)} %get-tuple-element.64), channel_id=1, source_target_pairs={{0,96},{32,64},{64,32},{96,0},{1,97},{33,65},{65,33},{97,1},{2,98}... | collective-permute-start | bytes 663560 | tf_op jit(solution)/shard_map/ppermute | solution.py:144
  137.0 10.5 %collective-permute-start.17 = (f32[432,128]{1,0:T(8,128)S(1)}, f32[432,128]{1,0:T(8,128)S(1)}, u32[]{:S(2)}, u32[]{:S(2)}) collective-permute-start(f32[432,128]{1,0:T(8,128)S(1)} %get-tuple-element.66), channel_id=1, source_target_pairs={{0,32},{32,0},{64,96},{96,64},{1,33},{33,1},{65,97},{97,65},{2,34}... | collective-permute-start | bytes 663560 | tf_op jit(solution)/shard_map/ppermute | solution.py:145
  137.0 11.2 %collective-permute-start.21 = (f32[432,128]{1,0:T(8,128)S(1)}, f32[432,128]{1,0:T(8,128)S(1)}, u32[]{:S(2)}, u32[]{:S(2)}) collective-permute-start(f32[432,128]{1,0:T(8,128)S(1)} %get-tuple-element.65), channel_id=1, source_target_pairs={{0,32},{32,0},{64,96},{96,64},{1,33},{33,1},{65,97},{97,65},{2,34}... | collective-permute-start | bytes 663560 | tf_op jit(solution)/shard_map/ppermute | solution.py:145
  147.4 11.0 %collective-permute-start.16 = (f32[864,128]{1,0:T(8,128)S(1)}, f32[864,128]{1,0:T(8,128)S(1)}, u32[]{:S(2)}, u32[]{:S(2)}) collective-permute-start(f32[864,128]{1,0:T(8,128)S(1)} %pad_maximum_fusion.1), channel_id=1, source_target_pairs={{0,32},{32,0},{64,96},{96,64},{1,33},{33,1},{65,97},{97,65},{2,34}... | collective-permute-start | bytes 1327112 | tf_op jit(solution)/shard_map/ppermute | solution.py:149
  148.3 11.6 %collective-permute-start.18 = (f32[864,128]{1,0:T(8,128)S(1)}, f32[864,128]{1,0:T(8,128)S(1)}, u32[]{:S(2)}, u32[]{:S(2)}) collective-permute-start(f32[864,128]{1,0:T(8,128)S(1)} %pad_maximum_fusion.2), channel_id=1, source_target_pairs={{0,96},{32,64},{64,32},{96,0},{1,97},{33,65},{65,33},{97,1},{2,98}... | collective-permute-start | bytes 1327112 | tf_op jit(solution)/shard_map/ppermute | solution.py:149
  150.7 17.2 %collective-permute-start.20 = (f32[864,128]{1,0:T(8,128)S(1)}, f32[864,128]{1,0:T(8,128)S(1)}, u32[]{:S(2)}, u32[]{:S(2)}) collective-permute-start(f32[864,128]{1,0:T(8,128)S(1)} %pad_maximum_fusion.3), channel_id=1, source_target_pairs={{0,32},{32,0},{64,96},{96,64},{1,33},{33,1},{65,97},{97,65},{2,34}... | collective-permute-start | bytes 1327112 | tf_op jit(solution)/shard_map/ppermute | solution.py:149
  151.1 18.3 %collective-permute-start.22 = (f32[864,128]{1,0:T(8,128)S(1)}, f32[864,128]{1,0:T(8,128)S(1)}, u32[]{:S(2)}, u32[]{:S(2)}) collective-permute-start(f32[864,128]{1,0:T(8,128)S(1)} %pad_maximum_fusion.4), channel_id=1, source_target_pairs={{0,96},{32,64},{64,32},{96,0},{1,97},{33,65},{65,33},{97,1},{2,98}... | collective-permute-start | bytes 1327112 | tf_op jit(solution)/shard_map/ppermute | solution.py:149
  191.4 7.5 %collective-permute-start.26 = (f32[8,16,1024]{2,1,0:T(8,128)S(1)}, f32[8,16,1024]{2,1,0:T(8,128)S(1)}, u32[]{:S(2)}, u32[]{:S(2)}) collective-permute-start(f32[8,16,1024]{2,1,0:T(8,128)S(1)} %convolution_select_fusion), channel_id=1, source_target_pairs={{0,16},{16,0},{1,17},{17,1},{2,18},{18,2},{3,19},{19,3},{4,20},{20... | collective-permute-start | bytes 1572872 | tf_op jit(solution)/shard_map/ppermute | solution.py:33
  200.0 12.2 %all-to-all-start.1 = ((f32[8,16,1024]{2,1,0:T(8,128)}), f32[8,16,1024]{2,1,0:T(8,128)S(1)}, u32[]{:S(2)}, u32[]{:S(2)}) async-start(f32[8,16,1024]{2,1,0:T(8,128)} %fusion.10), calls=%async_computation.1 | async-start | bytes 1048576 | tf_op jit(solution)/shard_map/all_to_all | solution.py:197
  (13 other events, 269.5 us)
Sparse Core Ops, SparseCore 0:
  9.8 111.2 all-gather.2

commit v2 on v1

--- a/solution.py
+++ b/solution.py
@@ -72,8 +72,8 @@
                 outs[2 * n + 1][...] = score[:, part:]
 
 
-def product(order, sides, blocks):
-    count, _, cols, width = blocks.shape
+def product(order, sides, blocks, first, count):
+    cols, width = blocks.shape[2:]
     part = sides[0].shape[0] // 4
     vmem = pl.BlockSpec(memory_space=pltpu.VMEM)
     return pl.pallas_call(
@@ -82,7 +82,7 @@
         out_shape=[jax.ShapeDtypeStruct((count * cols, part), F32)] * 4,
         in_specs=[pl.BlockSpec(memory_space=pltpu.SMEM)]
         + [vmem] * 5
-        + [pl.BlockSpec((1, 4, cols, width), lambda i: (i, 0, 0, 0))],
+        + [pl.BlockSpec((1, 4, cols, width), lambda i: (first + i, 0, 0, 0))],
         out_specs=[pl.BlockSpec((cols, part), lambda i: (i, 0))] * 4,
         compiler_params=pltpu.CompilerParams(vmem_limit_bytes=40 * 1024 * 1024),
     )(order, *sides, blocks)
@@ -138,9 +138,8 @@
     turn = (y >> 1) ^ (x & 1)
     order = (2 * turn + ((y & 1) ^ turn)).astype(jnp.int32).reshape(1)
     own = []
-    products = product(order, (s0, s1, s2a, s2b, s3), gathered)
     for n in (0, 2):
-        scores = [piece[n * cols : (n + 2) * cols] for piece in products]
+        scores = product(order, (s0, s1, s2a, s2b, s3), gathered, n, 2)
         to3 = lax.ppermute(scores[2][:cols], "x", flip(3))
         to1 = lax.ppermute(scores[2][cols:], "x", flip(1))
         part1 = jnp.concatenate([scores[1][:cols] + to3, scores[1][cols:]], 0)
@@ -154,7 +153,8 @@
     class_part = lax.dot_general(class_hot, terms, FIRST, preferred_element_type=F32)
     class_part = class_part[:, :quarter] + class_part[:, quarter : 2 * quarter] + class_part[:, 2 * quarter :]
     payload = jnp.concatenate([class_part, jnp.broadcast_to(top[None], (8, quarter))], axis=0)
-    payload = lax.all_to_all(jnp.broadcast_to(payload[None], (4,) + payload.shape), "y", 0, 0, tiled=True)
+    near = [payload] + [swap_y(payload, step) for step in (1, 2, 3)]
+    payload = jnp.stack([lax.select_n(y ^ place, *near) for place in range(4)])
     tops = payload[:, NCLASS]
     row_top = jnp.max(tops, axis=0)
     mass = jnp.sum(payload[:, :NCLASS] * jnp.exp(tops - row_top[None])[:, None, :], axis=0)

time: 221 us -> 218 us (0.986)
  blocking collectives: 10.3 us -> 0 us
  waiting for transfers between devices: 73 us -> 76.8 us
  Pallas kernels: 10.5 us -> 12.8 us
    all_to_all x1 -> x0, blocking collectives: 10.3 us -> none  [body(): lax.all_to_all(jnp.broadcast_to(payload[None], (4,) + payload.shape), 'y'...]
    ppermute x4 -> x7, waiting for transfers between devices: 11.5 us -> 17.2 us  [swap_y(): return lax.ppermute(block, 'y', flip(step))]
    ppermute x4 -> x7, starting transfers between devices: 9.91 us -> 13.9 us  [swap_y(): return lax.ppermute(block, 'y', flip(step))]
    ppermute x2, starting transfers between devices: 7.81 us -> 4.34 us  [swap_core(): return lax.ppermute(block, 'c', [(0, 1), (1, 0)])]
    ppermute x2, waiting for transfers between devices: 2.9 us -> 0.01 us  [body(): lax.ppermute(part3, 'x', flip(3))]
    ppermute x2, waiting for transfers between devices: 8.8 us -> 5.95 us  [body(): to3 = lax.ppermute(scores[2][:cols], 'x', flip(3))]
    ppermute x2, waiting for transfers between devices: 14.5 us -> 17.1 us  [body(): lax.ppermute(part1, 'x', flip(1))]
    pallas_call x1 -> x2, Pallas kernels: 10.5 us -> 12.8 us  [product(): pl.pallas_call(product_kernel, grid=(count,), out_shape=[jax.ShapeDtypeSt...]
  transfers between devices with their start and end apart: 29 -> 32, of which waited for: 23 -> 24; matrix products, arithmetic and copies ran while one was open for 6% -> 6% of each run, Pallas kernels for 0% -> 0%
where the time goes in v2:
time: 218 us; the launch traced here: 217 us
  starting transfers between devices  95.3 us (44%)
  waiting for transfers between devices  76.8 us (35%)
  between operations  14.6 us (7%)
  Pallas kernels  12.8 us (6%)
  matrix products  8.61 us (4%)
  other arithmetic  5.26 us (2%)
  local copies, waits for them, and re-layouts  4.02 us (2%)
    ppermute x4, starting transfers between devices, body(): lax.ppermute(parts[p], ('x', 'h', 'y'), image_moves(p))  25 us
    ppermute x7, waiting for transfers between devices, swap_y(): return lax.ppermute(block, 'y', flip(step))  17.2 us
    ppermute x2, waiting for transfers between devices, body(): lax.ppermute(part1, 'x', flip(1))  17.1 us
    ppermute x7, starting transfers between devices, swap_y(): return lax.ppermute(block, 'y', flip(step))  13.9 us
    pallas_call x2, Pallas kernels, product(): pl.pallas_call(product_kernel, grid=(count,), out_shape=[jax.ShapeDtypeSt...  12.8 us
    ppermute x1, starting transfers between devices, body(): norm = norm + lax.ppermute(norm, 'a', [(0, 1), (1, 0)])  12.1 us
    ppermute x1, starting transfers between devices, body(): norm = norm + lax.ppermute(norm, 'x', flip(2))  11.1 us
    ppermute x4, waiting for transfers between devices, body(): lax.ppermute(parts[p], ('x', 'h', 'y'), image_moves(p))  10.9 us
  transfers between devices with their start and end apart: 32, of which 24 were waited for; matrix products, arithmetic and copies ran while one was open for 6% of the time, Pallas kernels for 0%

profile of v2, /device:TPU:1, one launch (start us, length us, event | category | flops | bytes accessed | tf_op | source)
XLA Modules:
  0.0 217.3 jit_solution(1761222580624209923)
XLA Ops:
  11.1 8.8 %collective-permute-start.1 = (bf16[128,1024]{1,0:T(8,128)(2,1)S(1)}, bf16[128,1024]{1,0:T(8,128)(2,1)S(1)}, u32[]{:S(2)}, u32[]{:S(2)}) collective-permute-start(bf16[128,1024]{1,0:T(8,128)(2,1)S(1)} %get-tuple-element.63), channel_id=1, source_target_pairs={{0,4},{1,5},{2,38},{3,39},{4,68},{5,69},{6,102},{7,103},{8,7},{9,6... | collective-permute-start | bytes 786440 | tf_op jit(solution)/shard_map/ppermute | solution.py:107
  19.9 7.4 %collective-permute-start.2 = (bf16[128,1024]{1,0:T(8,128)(2,1)S(1)}, bf16[128,1024]{1,0:T(8,128)(2,1)S(1)}, u32[]{:S(2)}, u32[]{:S(2)}) collective-permute-start(bf16[128,1024]{1,0:T(8,128)(2,1)S(1)} %get-tuple-element.62), channel_id=1, source_target_pairs={{0,8},{1,9},{2,42},{3,43},{4,72},{5,73},{6,106},{7,107},{8,11},{9,... | collective-permute-start | bytes 786440 | tf_op jit(solution)/shard_map/ppermute | solution.py:107
  27.3 8.2 %collective-permute-start.3 = (bf16[128,1024]{1,0:T(8,128)(2,1)S(1)}, bf16[128,1024]{1,0:T(8,128)(2,1)S(1)}, u32[]{:S(2)}, u32[]{:S(2)}) collective-permute-start(bf16[128,1024]{1,0:T(8,128)(2,1)S(1)} %get-tuple-element.61), channel_id=1, source_target_pairs={{0,12},{1,13},{2,46},{3,47},{4,76},{5,77},{6,110},{7,111},{8,15},{... | collective-permute-start | bytes 786440 | tf_op jit(solution)/shard_map/ppermute | solution.py:107
  40.7 7.5 %collective-permute-done.2 = bf16[128,1024]{1,0:T(8,128)(2,1)S(1)} collective-permute-done((bf16[128,1024]{1,0:T(8,128)(2,1)S(1)}, bf16[128,1024]{1,0:T(8,128)(2,1)S(1)}, u32[]{:S(2)}, u32[]{:S(2)}) %collective-permute-start.2) | collective-permute-done | bytes 262176 | tf_op jit(solution)/shard_map/ppermute | solution.py:107
  48.2 3.4 %collective-permute-done.3 = bf16[128,1024]{1,0:T(8,128)(2,1)S(1)} collective-permute-done((bf16[128,1024]{1,0:T(8,128)(2,1)S(1)}, bf16[128,1024]{1,0:T(8,128)(2,1)S(1)}, u32[]{:S(2)}, u32[]{:S(2)}) %collective-permute-start.3) | collective-permute-done | bytes 262176 | tf_op jit(solution)/shard_map/ppermute | solution.py:107
  51.8 7.5 %collective-permute-start.5 = (bf16[512,1024]{1,0:T(8,128)(2,1)S(1)}, bf16[512,1024]{1,0:T(8,128)(2,1)S(1)}, u32[]{:S(2)}, u32[]{:S(2)}) collective-permute-start(bf16[512,1024]{1,0:T(8,128)(2,1)S(1)} %pad_maximum_fusion.s0), channel_id=1, source_target_pairs={{0,1},{1,0},{2,3},{3,2},{4,5},{5,4},{6,7},{7,6},{8,9},{9,8},{10,11... | collective-permute-start | bytes 3145736 | tf_op jit(solution)/shard_map/ppermute | solution.py:37
  63.4 11.1 %collective-permute-start.8 = (f32[16,432]{1,0:T(8,128)S(1)}, f32[16,432]{1,0:T(8,128)S(1)}, u32[]{:S(2)}, u32[]{:S(2)}) collective-permute-start(f32[16,432]{1,0:T(8,128)S(1)} %add.203), channel_id=1, source_target_pairs={{0,64},{32,96},{64,0},{96,32},{1,65},{33,97},{65,1},{97,33},{2,66}... | collective-permute-start | bytes 82952 | tf_op jit(solution)/shard_map/ppermute | solution.py:118
  75.9 3.9 %collective-permute-done.5.s1 = bf16[512,1024]{1,0:T(8,128)(2,1)S(1)} collective-permute-done((bf16[512,1024]{1,0:T(8,128)(2,1)S(1)}, bf16[512,1024]{1,0:T(8,128)(2,1)S(1)}, u32[]{:S(2)}, u32[]{:S(2)}) %collective-permute-start.5) | collective-permute-done | bytes 1048608 | tf_op jit(solution)/shard_map/ppermute | solution.py:37
  82.2 12.1 %collective-permute-start.11 = (f32[16,432]{1,0:T(8,128)S(1)}, f32[16,432]{1,0:T(8,128)S(1)}, u32[]{:S(2)}, u32[]{:S(2)}) collective-permute-start(f32[16,432]{1,0:T(8,128)S(1)} %add.204), channel_id=1, source_target_pairs={{0,128},{128,0},{1,129},{129,1},{2,130},{130,2},{3,131},{131,3},{4... | collective-permute-start | bytes 82952 | tf_op jit(solution)/shard_map/ppermute | solution.py:127
  99.0 3.4 %collective-permute-start.14 = (f32[24,432]{1,0:T(8,128)S(1)}, f32[24,432]{1,0:T(8,128)S(1)}, u32[]{:S(2)}, u32[]{:S(2)}) collective-permute-start(f32[24,432]{1,0:T(8,128)S(1)} %maximum_maximum_fusion), channel_id=1, source_target_pairs={{0,12},{4,8},{8,4},{12,0},{1,13},{5,9},{9,5},{13,1},{2,14},{6,10},... | collective-permute-start | bytes 124424 | tf_op jit(solution)/shard_map/ppermute | solution.py:129
  112.0 3.8 %collective-permute-done.10.s2b = bf16[256,1024]{1,0:T(8,128)(2,1)} collective-permute-done((bf16[256,1024]{1,0:T(8,128)(2,1)}, bf16[256,1024]{1,0:T(8,128)(2,1)}, u32[]{:S(2)}, u32[]{:S(2)}) %collective-permute-start.10) | collective-permute-done | bytes 524320 | tf_op jit(solution)/shard_map/ppermute | solution.py:37
  117.2 4.0 %all-gather.3.cloned.1.call-done = bf16[6912,1024]{1,0:T(8,128)(2,1)} async-done(((bf16[432,1024]{1,0:T(8,128)(2,1)}), bf16[6912,1024]{1,0:T(8,128)(2,1)}) %all-gather.3.cloned.1.call-update) | async-done | bytes 14155792 | tf_op jit(solution)/shard_map/all_gather | solution.py:101
  121.2 6.4 %shard_map.103 = (f32[864,128]{1,0:T(8,128)S(1)}, f32[864,128]{1,0:T(8,128)S(1)}, f32[864,128]{1,0:T(8,128)S(1)}, f32[864,128]{1,0:T(8,128)S(1)}) custom-call(s32[1]{0:T(128)} %bitcast.2.order, bf16[512,1024]{1,0:T(8,128)(2,1)S(1)} %pad_maximum_fusion.s0, bf16[512,1024]{1,0:T(8,128)(2,1)S(1)} %collective-permute-done.5.s1, ...), custom_call_target="tpu_custom_call" | custom-call | tf_op jit(solution)/shard_map/pallas_call | solution.py:79
  127.6 6.4 %shard_map.104 = (f32[864,128]{1,0:T(8,128)S(1)}, f32[864,128]{1,0:T(8,128)S(1)}, f32[864,128]{1,0:T(8,128)S(1)}, f32[864,128]{1,0:T(8,128)S(1)}) custom-call(s32[1]{0:T(128)} %bitcast.2.order, bf16[512,1024]{1,0:T(8,128)(2,1)S(1)} %pad_maximum_fusion.s0, bf16[512,1024]{1,0:T(8,128)(2,1)S(1)} %collective-permute-done.5.s1, ...), custom_call_target="tpu_custom_call" | custom-call | tf_op jit(solution)/shard_map/pallas_call | solution.py:79
  134.0 5.3 %collective-permute-start.15 = (f32[432,128]{1,0:T(8,128)S(1)}, f32[432,128]{1,0:T(8,128)S(1)}, u32[]{:S(2)}, u32[]{:S(2)}) collective-permute-start(f32[432,128]{1,0:T(8,128)S(1)} %get-tuple-element.78), channel_id=1, source_target_pairs={{0,96},{32,64},{64,32},{96,0},{1,97},{33,65},{65,33},{97,1},{2,98}... | collective-permute-start | bytes 663560 | tf_op jit(solution)/shard_map/ppermute | solution.py:143
  141.0 3.9 %collective-permute-done.15 = f32[432,128]{1,0:T(8,128)S(1)} collective-permute-done((f32[432,128]{1,0:T(8,128)S(1)}, f32[432,128]{1,0:T(8,128)S(1)}, u32[]{:S(2)}, u32[]{:S(2)}) %collective-permute-start.15) | collective-permute-done | bytes 221216 | tf_op jit(solution)/shard_map/ppermute | solution.py:143
  152.4 7.6 %collective-permute-done.16 = f32[864,128]{1,0:T(8,128)S(1)} collective-permute-done((f32[864,128]{1,0:T(8,128)S(1)}, f32[864,128]{1,0:T(8,128)S(1)}, u32[]{:S(2)}, u32[]{:S(2)}) %collective-permute-start.16) | collective-permute-done | bytes 442400 | tf_op jit(solution)/shard_map/ppermute | solution.py:148
  160.0 9.5 %collective-permute-done.20 = f32[864,128]{1,0:T(8,128)S(1)} collective-permute-done((f32[864,128]{1,0:T(8,128)S(1)}, f32[864,128]{1,0:T(8,128)S(1)}, u32[]{:S(2)}, u32[]{:S(2)}) %collective-permute-start.20) | collective-permute-done | bytes 442400 | tf_op jit(solution)/shard_map/ppermute | solution.py:148
  172.8 2.5 %collective-permute-start.24 = (f32[200,128]{1,0:T(8,128)S(1)}, f32[200,128]{1,0:T(8,128)S(1)}, u32[]{:S(2)}, u32[]{:S(2)}) collective-permute-start(f32[200,128]{1,0:T(8,128)S(1)} %pad_maximum_fusion.7), channel_id=1, source_target_pairs={{0,2},{1,3},{2,0},{3,1},{4,6},{5,7},{6,4},{7,5},{8,10},{9,11},{10,... | collective-permute-start | bytes 307208 | tf_op jit(solution)/shard_map/ppermute | solution.py:37
  175.5 3.3 %collective-permute-done.24 = f32[200,128]{1,0:T(8,128)S(1)} collective-permute-done((f32[200,128]{1,0:T(8,128)S(1)}, f32[200,128]{1,0:T(8,128)S(1)}, u32[]{:S(2)}, u32[]{:S(2)}) %collective-permute-start.24) | collective-permute-done | bytes 102432 | tf_op jit(solution)/shard_map/ppermute | solution.py:37
  181.8 2.9 %collective-permute-start.27 = (bf16[208,128]{1,0:T(8,128)(2,1)S(1)}, bf16[208,128]{1,0:T(8,128)(2,1)S(1)}, u32[]{:S(2)}, u32[]{:S(2)}) collective-permute-start(bf16[208,128]{1,0:T(8,128)(2,1)S(1)} %concatenate.58), channel_id=1, source_target_pairs={{0,8},{4,12},{8,0},{12,4},{1,9},{5,13},{9,1},{13,5},{2,10},{6,14},... | collective-permute-start | bytes 159752 | tf_op jit(solution)/shard_map/ppermute | solution.py:175
  184.7 2.8 %collective-permute-start.28 = (bf16[208,128]{1,0:T(8,128)(2,1)S(1)}, bf16[208,128]{1,0:T(8,128)(2,1)S(1)}, u32[]{:S(2)}, u32[]{:S(2)}) collective-permute-start(bf16[208,128]{1,0:T(8,128)(2,1)S(1)} %concatenate.58), channel_id=1, source_target_pairs={{0,12},{4,8},{8,4},{12,0},{1,13},{5,9},{9,5},{13,1},{2,14},{6,10},... | collective-permute-start | bytes 159752 | tf_op jit(solution)/shard_map/ppermute | solution.py:175
  196.7 4.2 %all-to-all-start = ((f32[8,16,1024]{2,1,0:T(8,128)}), f32[8,16,1024]{2,1,0:T(8,128)S(1)}, u32[]{:S(2)}, u32[]{:S(2)}) async-start(f32[8,16,1024]{2,1,0:T(8,128)} %fusion.10), calls=%async_computation | async-start | bytes 1048576 | tf_op jit(solution)/shard_map/all_to_all | solution.py:197
  201.5 7.6 %all-to-all-done = f32[8,16,1024]{2,1,0:T(8,128)S(1)} async-done(((f32[8,16,1024]{2,1,0:T(8,128)}), f32[8,16,1024]{2,1,0:T(8,128)S(1)}, u32[]{:S(2)}, u32[]{:S(2)}) %all-to-all-start) | async-done | bytes 524320 | tf_op jit(solution)/shard_map/all_to_all | solution.py:197
  (135 shorter events, 59.4 us)
Async XLA Ops:
  7.2 114.0 %all-gather.3.cloned.1.call-start = ((), (), s32[]{:S(2)}) async-start(), calls=%async_computation.1 | async-start | bytes 15040512 | tf_op jit(solution)/shard_map/all_gather | solution.py:101
  10.4 30.2 %collective-permute-start = (bf16[128,1024]{1,0:T(8,128)(2,1)S(1)}, bf16[128,1024]{1,0:T(8,128)(2,1)S(1)}, u32[]{:S(2)}, u32[]{:S(2)}) collective-permute-start(bf16[128,1024]{1,0:T(8,128)(2,1)S(1)} %get-tuple-element.64), channel_id=1, source_target_pairs={{0,0},{1,1},{2,34},{3,35},{4,64},{5,65},{6,98},{7,99},{8,3},{9,2},... | collective-permute-start | bytes 786440 | tf_op jit(solution)/shard_map/ppermute | solution.py:107
  11.1 29.6 %collective-permute-start.1 = (bf16[128,1024]{1,0:T(8,128)(2,1)S(1)}, bf16[128,1024]{1,0:T(8,128)(2,1)S(1)}, u32[]{:S(2)}, u32[]{:S(2)}) collective-permute-start(bf16[128,1024]{1,0:T(8,128)(2,1)S(1)} %get-tuple-element.63), channel_id=1, source_target_pairs={{0,4},{1,5},{2,38},{3,39},{4,68},{5,69},{6,102},{7,103},{8,7},{9,6... | collective-permute-start | bytes 786440 | tf_op jit(solution)/shard_map/ppermute | solution.py:107
  19.9 28.3 %collective-permute-start.2 = (bf16[128,1024]{1,0:T(8,128)(2,1)S(1)}, bf16[128,1024]{1,0:T(8,128)(2,1)S(1)}, u32[]{:S(2)}, u32[]{:S(2)}) collective-permute-start(bf16[128,1024]{1,0:T(8,128)(2,1)S(1)} %get-tuple-element.62), channel_id=1, source_target_pairs={{0,8},{1,9},{2,42},{3,43},{4,72},{5,73},{6,106},{7,107},{8,11},{9,... | collective-permute-start | bytes 786440 | tf_op jit(solution)/shard_map/ppermute | solution.py:107
  27.3 24.3 %collective-permute-start.3 = (bf16[128,1024]{1,0:T(8,128)(2,1)S(1)}, bf16[128,1024]{1,0:T(8,128)(2,1)S(1)}, u32[]{:S(2)}, u32[]{:S(2)}) collective-permute-start(bf16[128,1024]{1,0:T(8,128)(2,1)S(1)} %get-tuple-element.61), channel_id=1, source_target_pairs={{0,12},{1,13},{2,46},{3,47},{4,76},{5,77},{6,110},{7,111},{8,15},{... | collective-permute-start | bytes 786440 | tf_op jit(solution)/shard_map/ppermute | solution.py:107
  51.8 28.0 %collective-permute-start.5 = (bf16[512,1024]{1,0:T(8,128)(2,1)S(1)}, bf16[512,1024]{1,0:T(8,128)(2,1)S(1)}, u32[]{:S(2)}, u32[]{:S(2)}) collective-permute-start(bf16[512,1024]{1,0:T(8,128)(2,1)S(1)} %pad_maximum_fusion.s0), channel_id=1, source_target_pairs={{0,1},{1,0},{2,3},{3,2},{4,5},{5,4},{6,7},{7,6},{8,9},{9,8},{10,11... | collective-permute-start | bytes 3145736 | tf_op jit(solution)/shard_map/ppermute | solution.py:37
  59.3 22.8 %collective-permute-start.6 = (bf16[512,1024]{1,0:T(8,128)(2,1)S(1)}, bf16[512,1024]{1,0:T(8,128)(2,1)S(1)}, u32[]{:S(2)}, u32[]{:S(2)}) collective-permute-start(bf16[512,1024]{1,0:T(8,128)(2,1)S(1)} %pad_maximum_fusion.s0), channel_id=1, source_target_pairs={{0,3},{1,2},{2,1},{3,0},{4,7},{5,6},{6,5},{7,4},{8,11},{9,10},{10,... | collective-permute-start | bytes 3145736 | tf_op jit(solution)/shard_map/ppermute | solution.py:37
  63.4 12.5 %collective-permute-start.8 = (f32[16,432]{1,0:T(8,128)S(1)}, f32[16,432]{1,0:T(8,128)S(1)}, u32[]{:S(2)}, u32[]{:S(2)}) collective-permute-start(f32[16,432]{1,0:T(8,128)S(1)} %add.203), channel_id=1, source_target_pairs={{0,64},{32,96},{64,0},{96,32},{1,65},{33,97},{65,1},{97,33},{2,66}... | collective-permute-start | bytes 82952 | tf_op jit(solution)/shard_map/ppermute | solution.py:118
  82.2 14.5 %collective-permute-start.11 = (f32[16,432]{1,0:T(8,128)S(1)}, f32[16,432]{1,0:T(8,128)S(1)}, u32[]{:S(2)}, u32[]{:S(2)}) collective-permute-start(f32[16,432]{1,0:T(8,128)S(1)} %add.204), channel_id=1, source_target_pairs={{0,128},{128,0},{1,129},{129,1},{2,130},{130,2},{3,131},{131,3},{4... | collective-permute-start | bytes 82952 | tf_op jit(solution)/shard_map/ppermute | solution.py:127
  96.7 10.5 %collective-permute-start.12 = (f32[24,432]{1,0:T(8,128)S(1)}, f32[24,432]{1,0:T(8,128)S(1)}, u32[]{:S(2)}, u32[]{:S(2)}) collective-permute-start(f32[24,432]{1,0:T(8,128)S(1)} %maximum_maximum_fusion), channel_id=1, source_target_pairs={{0,4},{4,0},{8,12},{12,8},{1,5},{5,1},{9,13},{13,9},{2,6},{6,2},{1... | collective-permute-start | bytes 124424 | tf_op jit(solution)/shard_map/ppermute | solution.py:129
  96.8 10.5 %collective-permute-start.13 = (f32[24,432]{1,0:T(8,128)S(1)}, f32[24,432]{1,0:T(8,128)S(1)}, u32[]{:S(2)}, u32[]{:S(2)}) collective-permute-start(f32[24,432]{1,0:T(8,128)S(1)} %maximum_maximum_fusion), channel_id=1, source_target_pairs={{0,8},{4,12},{8,0},{12,4},{1,9},{5,13},{9,1},{13,5},{2,10},{6,14},... | collective-permute-start | bytes 124424 | tf_op jit(solution)/shard_map/ppermute | solution.py:129
  99.0 9.5 %collective-permute-start.14 = (f32[24,432]{1,0:T(8,128)S(1)}, f32[24,432]{1,0:T(8,128)S(1)}, u32[]{:S(2)}, u32[]{:S(2)}) collective-permute-start(f32[24,432]{1,0:T(8,128)S(1)} %maximum_maximum_fusion), channel_id=1, source_target_pairs={{0,12},{4,8},{8,4},{12,0},{1,13},{5,9},{9,5},{13,1},{2,14},{6,10},... | collective-permute-start | bytes 124424 | tf_op jit(solution)/shard_map/ppermute | solution.py:129
  104.0 11.7 %collective-permute-start.10 = (bf16[256,1024]{1,0:T(8,128)(2,1)}, bf16[256,1024]{1,0:T(8,128)(2,1)}, u32[]{:S(2)}, u32[]{:S(2)}) collective-permute-start(bf16[256,1024]{1,0:T(8,128)(2,1)} %slice.191), channel_id=1, source_target_pairs={{0,3},{1,2},{2,1},{3,0},{4,7},{5,6},{6,5},{7,4},{8,11},{9,10},{10,... | collective-permute-start | bytes 1572872 | tf_op jit(solution)/shard_map/ppermute | solution.py:37
  107.2 10.0 %collective-permute-start.9 = (bf16[256,1024]{1,0:T(8,128)(2,1)}, bf16[256,1024]{1,0:T(8,128)(2,1)}, u32[]{:S(2)}, u32[]{:S(2)}) collective-permute-start(bf16[256,1024]{1,0:T(8,128)(2,1)} %slice.190), channel_id=1, source_target_pairs={{0,1},{1,0},{2,3},{3,2},{4,5},{5,4},{6,7},{7,6},{8,9},{9,8},{10,11... | collective-permute-start | bytes 1572872 | tf_op jit(solution)/shard_map/ppermute | solution.py:37
  134.0 11.0 %collective-permute-start.15 = (f32[432,128]{1,0:T(8,128)S(1)}, f32[432,128]{1,0:T(8,128)S(1)}, u32[]{:S(2)}, u32[]{:S(2)}) collective-permute-start(f32[432,128]{1,0:T(8,128)S(1)} %get-tuple-element.78), channel_id=1, source_target_pairs={{0,96},{32,64},{64,32},{96,0},{1,97},{33,65},{65,33},{97,1},{2,98}... | collective-permute-start | bytes 663560 | tf_op jit(solution)/shard_map/ppermute | solution.py:143
  139.4 6.5 %collective-permute-start.17 = (f32[432,128]{1,0:T(8,128)S(1)}, f32[432,128]{1,0:T(8,128)S(1)}, u32[]{:S(2)}, u32[]{:S(2)}) collective-permute-start(f32[432,128]{1,0:T(8,128)S(1)} %get-tuple-element.79), channel_id=1, source_target_pairs={{0,32},{32,0},{64,96},{96,64},{1,33},{33,1},{65,97},{97,65},{2,34}... | collective-permute-start | bytes 663560 | tf_op jit(solution)/shard_map/ppermute | solution.py:144
  139.4 10.3 %collective-permute-start.19 = (f32[432,128]{1,0:T(8,128)S(1)}, f32[432,128]{1,0:T(8,128)S(1)}, u32[]{:S(2)}, u32[]{:S(2)}) collective-permute-start(f32[432,128]{1,0:T(8,128)S(1)} %get-tuple-element.72), channel_id=1, source_target_pairs={{0,96},{32,64},{64,32},{96,0},{1,97},{33,65},{65,33},{97,1},{2,98}... | collective-permute-start | bytes 663560 | tf_op jit(solution)/shard_map/ppermute | solution.py:143
  140.2 10.3 %collective-permute-start.21 = (f32[432,128]{1,0:T(8,128)S(1)}, f32[432,128]{1,0:T(8,128)S(1)}, u32[]{:S(2)}, u32[]{:S(2)}) collective-permute-start(f32[432,128]{1,0:T(8,128)S(1)} %get-tuple-element.73), channel_id=1, source_target_pairs={{0,32},{32,0},{64,96},{96,64},{1,33},{33,1},{65,97},{97,65},{2,34}... | collective-permute-start | bytes 663560 | tf_op jit(solution)/shard_map/ppermute | solution.py:144
  145.1 15.0 %collective-permute-start.16 = (f32[864,128]{1,0:T(8,128)S(1)}, f32[864,128]{1,0:T(8,128)S(1)}, u32[]{:S(2)}, u32[]{:S(2)}) collective-permute-start(f32[864,128]{1,0:T(8,128)S(1)} %pad_maximum_fusion.1), channel_id=1, source_target_pairs={{0,32},{32,0},{64,96},{96,64},{1,33},{33,1},{65,97},{97,65},{2,34}... | collective-permute-start | bytes 1327112 | tf_op jit(solution)/shard_map/ppermute | solution.py:148
  145.9 14.1 %collective-permute-start.18 = (f32[864,128]{1,0:T(8,128)S(1)}, f32[864,128]{1,0:T(8,128)S(1)}, u32[]{:S(2)}, u32[]{:S(2)}) collective-permute-start(f32[864,128]{1,0:T(8,128)S(1)} %pad_maximum_fusion.2), channel_id=1, source_target_pairs={{0,96},{32,64},{64,32},{96,0},{1,97},{33,65},{65,33},{97,1},{2,98}... | collective-permute-start | bytes 1327112 | tf_op jit(solution)/shard_map/ppermute | solution.py:148
  149.8 19.7 %collective-permute-start.20 = (f32[864,128]{1,0:T(8,128)S(1)}, f32[864,128]{1,0:T(8,128)S(1)}, u32[]{:S(2)}, u32[]{:S(2)}) collective-permute-start(f32[864,128]{1,0:T(8,128)S(1)} %pad_maximum_fusion.3), channel_id=1, source_target_pairs={{0,32},{32,0},{64,96},{96,64},{1,33},{33,1},{65,97},{97,65},{2,34}... | collective-permute-start | bytes 1327112 | tf_op jit(solution)/shard_map/ppermute | solution.py:148
  150.6 18.9 %collective-permute-start.22 = (f32[864,128]{1,0:T(8,128)S(1)}, f32[864,128]{1,0:T(8,128)S(1)}, u32[]{:S(2)}, u32[]{:S(2)}) collective-permute-start(f32[864,128]{1,0:T(8,128)S(1)} %pad_maximum_fusion.4), channel_id=1, source_target_pairs={{0,96},{32,64},{64,32},{96,0},{1,97},{33,65},{65,33},{97,1},{2,98}... | collective-permute-start | bytes 1327112 | tf_op jit(solution)/shard_map/ppermute | solution.py:148
  181.8 7.2 %collective-permute-start.27 = (bf16[208,128]{1,0:T(8,128)(2,1)S(1)}, bf16[208,128]{1,0:T(8,128)(2,1)S(1)}, u32[]{:S(2)}, u32[]{:S(2)}) collective-permute-start(bf16[208,128]{1,0:T(8,128)(2,1)S(1)} %concatenate.58), channel_id=1, source_target_pairs={{0,8},{4,12},{8,0},{12,4},{1,9},{5,13},{9,1},{13,5},{2,10},{6,14},... | collective-permute-start | bytes 159752 | tf_op jit(solution)/shard_map/ppermute | solution.py:175
  196.7 12.4 %all-to-all-start = ((f32[8,16,1024]{2,1,0:T(8,128)}), f32[8,16,1024]{2,1,0:T(8,128)S(1)}, u32[]{:S(2)}, u32[]{:S(2)}) async-start(f32[8,16,1024]{2,1,0:T(8,128)} %fusion.10), calls=%async_computation | async-start | bytes 1048576 | tf_op jit(solution)/shard_map/all_to_all | solution.py:197
  (16 other events, 275.9 us)
Sparse Core Ops, SparseCore 0:
  9.8 111.2 all-gather.2

commit v3 on v2

--- a/solution.py
+++ b/solution.py
@@ -194,8 +194,13 @@
         return jnp.where(place == owned, count_row[None, None], sums)
 
     outgoing = sums_of(c) + swap_core(sums_of(1 - c))
-    arrived = jnp.sum(lax.all_to_all(outgoing, ("a", "x"), 0, 0, tiled=True), axis=0)
-    counts = arrived[owned, :NCLASS]
+    place = lax.broadcasted_iota(jnp.int32, outgoing.shape, 1)
+    pieces = [piece[:, owned : owned + 1].astype(F32) for piece in split3(outgoing)]
+    for n in (1, 2):
+        outgoing = jnp.where(place == owned + n, pieces[n], outgoing)
+    arrived = lax.all_to_all(outgoing.astype(BF16), ("a", "x"), 0, 0, tiled=True).astype(F32)
+    arrived = jnp.sum(arrived, axis=0)
+    counts = jnp.sum(arrived[owned : owned + 3, :NCLASS], axis=0)
     own_counts = lax.dynamic_slice_in_dim(counts, img_place * owned, owned, 0)
     class_avg = arrived[:owned] / (own_counts[:, None] + 1.0)
     occupancy = counts * (NCLASS / (rows * 16))

time: 218 us -> 216 us (level)
  no operation moved by 1% of the time
where the time goes in v3:
time: 216 us
  starting transfers between devices  95.3 us (44%)
  waiting for transfers between devices  74.8 us (35%)
  between operations  14.6 us (7%)
  Pallas kernels  12.8 us (6%)
  matrix products  7.81 us (4%)
  other arithmetic  6.15 us (3%)
  local copies, waits for them, and re-layouts  4.05 us (2%)
    ppermute x4, starting transfers between devices, body(): lax.ppermute(parts[p], ('x', 'h', 'y'), image_moves(p))  25 us
    ppermute x7, waiting for transfers between devices, swap_y(): return lax.ppermute(block, 'y', flip(step))  17.1 us
    ppermute x2, waiting for transfers between devices, body(): lax.ppermute(part1, 'x', flip(1))  17.1 us
    ppermute x7, starting transfers between devices, swap_y(): return lax.ppermute(block, 'y', flip(step))  13.9 us
    pallas_call x2, Pallas kernels, product(): pl.pallas_call(product_kernel, grid=(count,), out_shape=[jax.ShapeDtypeSt...  12.8 us
    ppermute x1, starting transfers between devices, body(): norm = norm + lax.ppermute(norm, 'a', [(0, 1), (1, 0)])  12.1 us
    ppermute x1, starting transfers between devices, body(): norm = norm + lax.ppermute(norm, 'x', flip(2))  11.1 us
    ppermute x4, waiting for transfers between devices, body(): lax.ppermute(parts[p], ('x', 'h', 'y'), image_moves(p))  10.9 us
  transfers between devices with their start and end apart: 32, of which 24 were waited for; matrix products, arithmetic and copies ran while one was open for 6% of the time, Pallas kernels for 0%

profile of v3, /device:TPU:1, one launch (start us, length us, event | category | flops | bytes accessed | tf_op | source)
XLA Modules:
  0.0 215.5 jit_solution(9935092894956698092)
XLA Ops:
  11.1 8.8 %collective-permute-start.1 = (bf16[128,1024]{1,0:T(8,128)(2,1)S(1)}, bf16[128,1024]{1,0:T(8,128)(2,1)S(1)}, u32[]{:S(2)}, u32[]{:S(2)}) collective-permute-start(bf16[128,1024]{1,0:T(8,128)(2,1)S(1)} %get-tuple-element.63), channel_id=1, source_target_pairs={{0,4},{1,5},{2,38},{3,39},{4,68},{5,69},{6,102},{7,103},{8,7},{9,6... | collective-permute-start | bytes 786440 | tf_op jit(solution)/shard_map/ppermute | solution.py:107
  19.9 7.4 %collective-permute-start.2 = (bf16[128,1024]{1,0:T(8,128)(2,1)S(1)}, bf16[128,1024]{1,0:T(8,128)(2,1)S(1)}, u32[]{:S(2)}, u32[]{:S(2)}) collective-permute-start(bf16[128,1024]{1,0:T(8,128)(2,1)S(1)} %get-tuple-element.62), channel_id=1, source_target_pairs={{0,8},{1,9},{2,42},{3,43},{4,72},{5,73},{6,106},{7,107},{8,11},{9,... | collective-permute-start | bytes 786440 | tf_op jit(solution)/shard_map/ppermute | solution.py:107
  27.3 8.2 %collective-permute-start.3 = (bf16[128,1024]{1,0:T(8,128)(2,1)S(1)}, bf16[128,1024]{1,0:T(8,128)(2,1)S(1)}, u32[]{:S(2)}, u32[]{:S(2)}) collective-permute-start(bf16[128,1024]{1,0:T(8,128)(2,1)S(1)} %get-tuple-element.61), channel_id=1, source_target_pairs={{0,12},{1,13},{2,46},{3,47},{4,76},{5,77},{6,110},{7,111},{8,15},{... | collective-permute-start | bytes 786440 | tf_op jit(solution)/shard_map/ppermute | solution.py:107
  40.7 7.5 %collective-permute-done.2 = bf16[128,1024]{1,0:T(8,128)(2,1)S(1)} collective-permute-done((bf16[128,1024]{1,0:T(8,128)(2,1)S(1)}, bf16[128,1024]{1,0:T(8,128)(2,1)S(1)}, u32[]{:S(2)}, u32[]{:S(2)}) %collective-permute-start.2) | collective-permute-done | bytes 262176 | tf_op jit(solution)/shard_map/ppermute | solution.py:107
  48.2 3.4 %collective-permute-done.3 = bf16[128,1024]{1,0:T(8,128)(2,1)S(1)} collective-permute-done((bf16[128,1024]{1,0:T(8,128)(2,1)S(1)}, bf16[128,1024]{1,0:T(8,128)(2,1)S(1)}, u32[]{:S(2)}, u32[]{:S(2)}) %collective-permute-start.3) | collective-permute-done | bytes 262176 | tf_op jit(solution)/shard_map/ppermute | solution.py:107
  51.8 7.5 %collective-permute-start.5 = (bf16[512,1024]{1,0:T(8,128)(2,1)S(1)}, bf16[512,1024]{1,0:T(8,128)(2,1)S(1)}, u32[]{:S(2)}, u32[]{:S(2)}) collective-permute-start(bf16[512,1024]{1,0:T(8,128)(2,1)S(1)} %pad_maximum_fusion.s0), channel_id=1, source_target_pairs={{0,1},{1,0},{2,3},{3,2},{4,5},{5,4},{6,7},{7,6},{8,9},{9,8},{10,11... | collective-permute-start | bytes 3145736 | tf_op jit(solution)/shard_map/ppermute | solution.py:37
  63.4 11.1 %collective-permute-start.8 = (f32[16,432]{1,0:T(8,128)S(1)}, f32[16,432]{1,0:T(8,128)S(1)}, u32[]{:S(2)}, u32[]{:S(2)}) collective-permute-start(f32[16,432]{1,0:T(8,128)S(1)} %add.196), channel_id=1, source_target_pairs={{0,64},{32,96},{64,0},{96,32},{1,65},{33,97},{65,1},{97,33},{2,66}... | collective-permute-start | bytes 82952 | tf_op jit(solution)/shard_map/ppermute | solution.py:118
  75.9 3.9 %collective-permute-done.5.s1 = bf16[512,1024]{1,0:T(8,128)(2,1)S(1)} collective-permute-done((bf16[512,1024]{1,0:T(8,128)(2,1)S(1)}, bf16[512,1024]{1,0:T(8,128)(2,1)S(1)}, u32[]{:S(2)}, u32[]{:S(2)}) %collective-permute-start.5) | collective-permute-done | bytes 1048608 | tf_op jit(solution)/shard_map/ppermute | solution.py:37
  82.2 12.1 %collective-permute-start.11 = (f32[16,432]{1,0:T(8,128)S(1)}, f32[16,432]{1,0:T(8,128)S(1)}, u32[]{:S(2)}, u32[]{:S(2)}) collective-permute-start(f32[16,432]{1,0:T(8,128)S(1)} %add.197), channel_id=1, source_target_pairs={{0,128},{128,0},{1,129},{129,1},{2,130},{130,2},{3,131},{131,3},{4... | collective-permute-start | bytes 82952 | tf_op jit(solution)/shard_map/ppermute | solution.py:127
  99.0 3.4 %collective-permute-start.14 = (f32[24,432]{1,0:T(8,128)S(1)}, f32[24,432]{1,0:T(8,128)S(1)}, u32[]{:S(2)}, u32[]{:S(2)}) collective-permute-start(f32[24,432]{1,0:T(8,128)S(1)} %maximum_maximum_fusion), channel_id=1, source_target_pairs={{0,12},{4,8},{8,4},{12,0},{1,13},{5,9},{9,5},{13,1},{2,14},{6,10},... | collective-permute-start | bytes 124424 | tf_op jit(solution)/shard_map/ppermute | solution.py:129
  112.0 3.8 %collective-permute-done.10.s2b = bf16[256,1024]{1,0:T(8,128)(2,1)} collective-permute-done((bf16[256,1024]{1,0:T(8,128)(2,1)}, bf16[256,1024]{1,0:T(8,128)(2,1)}, u32[]{:S(2)}, u32[]{:S(2)}) %collective-permute-start.10) | collective-permute-done | bytes 524320 | tf_op jit(solution)/shard_map/ppermute | solution.py:37
  117.2 4.0 %all-gather.3.cloned.1.call-done = bf16[6912,1024]{1,0:T(8,128)(2,1)} async-done(((bf16[432,1024]{1,0:T(8,128)(2,1)}), bf16[6912,1024]{1,0:T(8,128)(2,1)}) %all-gather.3.cloned.1.call-update) | async-done | bytes 14155792 | tf_op jit(solution)/shard_map/all_gather | solution.py:101
  121.2 6.4 %shard_map.103 = (f32[864,128]{1,0:T(8,128)S(1)}, f32[864,128]{1,0:T(8,128)S(1)}, f32[864,128]{1,0:T(8,128)S(1)}, f32[864,128]{1,0:T(8,128)S(1)}) custom-call(s32[1]{0:T(128)} %bitcast.2.order, bf16[512,1024]{1,0:T(8,128)(2,1)S(1)} %pad_maximum_fusion.s0, bf16[512,1024]{1,0:T(8,128)(2,1)S(1)} %collective-permute-done.5.s1, ...), custom_call_target="tpu_custom_call" | custom-call | tf_op jit(solution)/shard_map/pallas_call | solution.py:79
  127.6 6.4 %shard_map.104 = (f32[864,128]{1,0:T(8,128)S(1)}, f32[864,128]{1,0:T(8,128)S(1)}, f32[864,128]{1,0:T(8,128)S(1)}, f32[864,128]{1,0:T(8,128)S(1)}) custom-call(s32[1]{0:T(128)} %bitcast.2.order, bf16[512,1024]{1,0:T(8,128)(2,1)S(1)} %pad_maximum_fusion.s0, bf16[512,1024]{1,0:T(8,128)(2,1)S(1)} %collective-permute-done.5.s1, ...), custom_call_target="tpu_custom_call" | custom-call | tf_op jit(solution)/shard_map/pallas_call | solution.py:79
  134.0 5.3 %collective-permute-start.15 = (f32[432,128]{1,0:T(8,128)S(1)}, f32[432,128]{1,0:T(8,128)S(1)}, u32[]{:S(2)}, u32[]{:S(2)}) collective-permute-start(f32[432,128]{1,0:T(8,128)S(1)} %get-tuple-element.80), channel_id=1, source_target_pairs={{0,96},{32,64},{64,32},{96,0},{1,97},{33,65},{65,33},{97,1},{2,98}... | collective-permute-start | bytes 663560 | tf_op jit(solution)/shard_map/ppermute | solution.py:143
  141.0 3.9 %collective-permute-done.15 = f32[432,128]{1,0:T(8,128)S(1)} collective-permute-done((f32[432,128]{1,0:T(8,128)S(1)}, f32[432,128]{1,0:T(8,128)S(1)}, u32[]{:S(2)}, u32[]{:S(2)}) %collective-permute-start.15) | collective-permute-done | bytes 221216 | tf_op jit(solution)/shard_map/ppermute | solution.py:143
  152.4 7.6 %collective-permute-done.16 = f32[864,128]{1,0:T(8,128)S(1)} collective-permute-done((f32[864,128]{1,0:T(8,128)S(1)}, f32[864,128]{1,0:T(8,128)S(1)}, u32[]{:S(2)}, u32[]{:S(2)}) %collective-permute-start.16) | collective-permute-done | bytes 442400 | tf_op jit(solution)/shard_map/ppermute | solution.py:148
  160.0 9.5 %collective-permute-done.20 = f32[864,128]{1,0:T(8,128)S(1)} collective-permute-done((f32[864,128]{1,0:T(8,128)S(1)}, f32[864,128]{1,0:T(8,128)S(1)}, u32[]{:S(2)}, u32[]{:S(2)}) %collective-permute-start.20) | collective-permute-done | bytes 442400 | tf_op jit(solution)/shard_map/ppermute | solution.py:148
  172.8 2.5 %collective-permute-start.24 = (f32[200,128]{1,0:T(8,128)S(1)}, f32[200,128]{1,0:T(8,128)S(1)}, u32[]{:S(2)}, u32[]{:S(2)}) collective-permute-start(f32[200,128]{1,0:T(8,128)S(1)} %pad_maximum_fusion.7), channel_id=1, source_target_pairs={{0,2},{1,3},{2,0},{3,1},{4,6},{5,7},{6,4},{7,5},{8,10},{9,11},{10,... | collective-permute-start | bytes 307208 | tf_op jit(solution)/shard_map/ppermute | solution.py:37
  175.5 3.3 %collective-permute-done.24 = f32[200,128]{1,0:T(8,128)S(1)} collective-permute-done((f32[200,128]{1,0:T(8,128)S(1)}, f32[200,128]{1,0:T(8,128)S(1)}, u32[]{:S(2)}, u32[]{:S(2)}) %collective-permute-start.24) | collective-permute-done | bytes 102432 | tf_op jit(solution)/shard_map/ppermute | solution.py:37
  181.8 2.9 %collective-permute-start.27 = (bf16[208,128]{1,0:T(8,128)(2,1)S(1)}, bf16[208,128]{1,0:T(8,128)(2,1)S(1)}, u32[]{:S(2)}, u32[]{:S(2)}) collective-permute-start(bf16[208,128]{1,0:T(8,128)(2,1)S(1)} %concatenate.58), channel_id=1, source_target_pairs={{0,8},{4,12},{8,0},{12,4},{1,9},{5,13},{9,1},{13,5},{2,10},{6,14},... | collective-permute-start | bytes 159752 | tf_op jit(solution)/shard_map/ppermute | solution.py:175
  184.7 2.8 %collective-permute-start.28 = (bf16[208,128]{1,0:T(8,128)(2,1)S(1)}, bf16[208,128]{1,0:T(8,128)(2,1)S(1)}, u32[]{:S(2)}, u32[]{:S(2)}) collective-permute-start(bf16[208,128]{1,0:T(8,128)(2,1)S(1)} %concatenate.58), channel_id=1, source_target_pairs={{0,12},{4,8},{8,4},{12,0},{1,13},{5,9},{9,5},{13,1},{2,14},{6,10},... | collective-permute-start | bytes 159752 | tf_op jit(solution)/shard_map/ppermute | solution.py:175
  196.8 4.2 %all-to-all-start = ((bf16[8,16,1024]{2,1,0:T(8,128)(2,1)}), bf16[8,16,1024]{2,1,0:T(8,128)(2,1)S(1)}, u32[]{:S(2)}, u32[]{:S(2)}) async-start(bf16[8,16,1024]{2,1,0:T(8,128)(2,1)} %select_convert_fusion), calls=%async_computation | async-start | bytes 524288 | tf_op jit(solution)/shard_map/all_to_all | solution.py:201
  201.7 5.6 %all-to-all-done = bf16[8,16,1024]{2,1,0:T(8,128)(2,1)S(1)} async-done(((bf16[8,16,1024]{2,1,0:T(8,128)(2,1)}), bf16[8,16,1024]{2,1,0:T(8,128)(2,1)S(1)}, u32[]{:S(2)}, u32[]{:S(2)}) %all-to-all-start) | async-done | bytes 262176 | tf_op jit(solution)/shard_map/all_to_all | solution.py:201
  (141 shorter events, 59.6 us)
Async XLA Ops:
  7.2 114.0 %all-gather.3.cloned.1.call-start = ((), (), s32[]{:S(2)}) async-start(), calls=%async_computation.1 | async-start | bytes 15040512 | tf_op jit(solution)/shard_map/all_gather | solution.py:101
  10.4 30.2 %collective-permute-start = (bf16[128,1024]{1,0:T(8,128)(2,1)S(1)}, bf16[128,1024]{1,0:T(8,128)(2,1)S(1)}, u32[]{:S(2)}, u32[]{:S(2)}) collective-permute-start(bf16[128,1024]{1,0:T(8,128)(2,1)S(1)} %get-tuple-element.64), channel_id=1, source_target_pairs={{0,0},{1,1},{2,34},{3,35},{4,64},{5,65},{6,98},{7,99},{8,3},{9,2},... | collective-permute-start | bytes 786440 | tf_op jit(solution)/shard_map/ppermute | solution.py:107
  11.1 29.6 %collective-permute-start.1 = (bf16[128,1024]{1,0:T(8,128)(2,1)S(1)}, bf16[128,1024]{1,0:T(8,128)(2,1)S(1)}, u32[]{:S(2)}, u32[]{:S(2)}) collective-permute-start(bf16[128,1024]{1,0:T(8,128)(2,1)S(1)} %get-tuple-element.63), channel_id=1, source_target_pairs={{0,4},{1,5},{2,38},{3,39},{4,68},{5,69},{6,102},{7,103},{8,7},{9,6... | collective-permute-start | bytes 786440 | tf_op jit(solution)/shard_map/ppermute | solution.py:107
  19.9 28.3 %collective-permute-start.2 = (bf16[128,1024]{1,0:T(8,128)(2,1)S(1)}, bf16[128,1024]{1,0:T(8,128)(2,1)S(1)}, u32[]{:S(2)}, u32[]{:S(2)}) collective-permute-start(bf16[128,1024]{1,0:T(8,128)(2,1)S(1)} %get-tuple-element.62), channel_id=1, source_target_pairs={{0,8},{1,9},{2,42},{3,43},{4,72},{5,73},{6,106},{7,107},{8,11},{9,... | collective-permute-start | bytes 786440 | tf_op jit(solution)/shard_map/ppermute | solution.py:107
  27.3 24.3 %collective-permute-start.3 = (bf16[128,1024]{1,0:T(8,128)(2,1)S(1)}, bf16[128,1024]{1,0:T(8,128)(2,1)S(1)}, u32[]{:S(2)}, u32[]{:S(2)}) collective-permute-start(bf16[128,1024]{1,0:T(8,128)(2,1)S(1)} %get-tuple-element.61), channel_id=1, source_target_pairs={{0,12},{1,13},{2,46},{3,47},{4,76},{5,77},{6,110},{7,111},{8,15},{... | collective-permute-start | bytes 786440 | tf_op jit(solution)/shard_map/ppermute | solution.py:107
  51.8 28.0 %collective-permute-start.5 = (bf16[512,1024]{1,0:T(8,128)(2,1)S(1)}, bf16[512,1024]{1,0:T(8,128)(2,1)S(1)}, u32[]{:S(2)}, u32[]{:S(2)}) collective-permute-start(bf16[512,1024]{1,0:T(8,128)(2,1)S(1)} %pad_maximum_fusion.s0), channel_id=1, source_target_pairs={{0,1},{1,0},{2,3},{3,2},{4,5},{5,4},{6,7},{7,6},{8,9},{9,8},{10,11... | collective-permute-start | bytes 3145736 | tf_op jit(solution)/shard_map/ppermute | solution.py:37
  59.3 22.8 %collective-permute-start.6 = (bf16[512,1024]{1,0:T(8,128)(2,1)S(1)}, bf16[512,1024]{1,0:T(8,128)(2,1)S(1)}, u32[]{:S(2)}, u32[]{:S(2)}) collective-permute-start(bf16[512,1024]{1,0:T(8,128)(2,1)S(1)} %pad_maximum_fusion.s0), channel_id=1, source_target_pairs={{0,3},{1,2},{2,1},{3,0},{4,7},{5,6},{6,5},{7,4},{8,11},{9,10},{10,... | collective-permute-start | bytes 3145736 | tf_op jit(solution)/shard_map/ppermute | solution.py:37
  63.4 12.5 %collective-permute-start.8 = (f32[16,432]{1,0:T(8,128)S(1)}, f32[16,432]{1,0:T(8,128)S(1)}, u32[]{:S(2)}, u32[]{:S(2)}) collective-permute-start(f32[16,432]{1,0:T(8,128)S(1)} %add.196), channel_id=1, source_target_pairs={{0,64},{32,96},{64,0},{96,32},{1,65},{33,97},{65,1},{97,33},{2,66}... | collective-permute-start | bytes 82952 | tf_op jit(solution)/shard_map/ppermute | solution.py:118
  82.2 14.5 %collective-permute-start.11 = (f32[16,432]{1,0:T(8,128)S(1)}, f32[16,432]{1,0:T(8,128)S(1)}, u32[]{:S(2)}, u32[]{:S(2)}) collective-permute-start(f32[16,432]{1,0:T(8,128)S(1)} %add.197), channel_id=1, source_target_pairs={{0,128},{128,0},{1,129},{129,1},{2,130},{130,2},{3,131},{131,3},{4... | collective-permute-start | bytes 82952 | tf_op jit(solution)/shard_map/ppermute | solution.py:127
  96.7 10.5 %collective-permute-start.12 = (f32[24,432]{1,0:T(8,128)S(1)}, f32[24,432]{1,0:T(8,128)S(1)}, u32[]{:S(2)}, u32[]{:S(2)}) collective-permute-start(f32[24,432]{1,0:T(8,128)S(1)} %maximum_maximum_fusion), channel_id=1, source_target_pairs={{0,4},{4,0},{8,12},{12,8},{1,5},{5,1},{9,13},{13,9},{2,6},{6,2},{1... | collective-permute-start | bytes 124424 | tf_op jit(solution)/shard_map/ppermute | solution.py:129
  96.8 10.5 %collective-permute-start.13 = (f32[24,432]{1,0:T(8,128)S(1)}, f32[24,432]{1,0:T(8,128)S(1)}, u32[]{:S(2)}, u32[]{:S(2)}) collective-permute-start(f32[24,432]{1,0:T(8,128)S(1)} %maximum_maximum_fusion), channel_id=1, source_target_pairs={{0,8},{4,12},{8,0},{12,4},{1,9},{5,13},{9,1},{13,5},{2,10},{6,14},... | collective-permute-start | bytes 124424 | tf_op jit(solution)/shard_map/ppermute | solution.py:129
  99.0 9.5 %collective-permute-start.14 = (f32[24,432]{1,0:T(8,128)S(1)}, f32[24,432]{1,0:T(8,128)S(1)}, u32[]{:S(2)}, u32[]{:S(2)}) collective-permute-start(f32[24,432]{1,0:T(8,128)S(1)} %maximum_maximum_fusion), channel_id=1, source_target_pairs={{0,12},{4,8},{8,4},{12,0},{1,13},{5,9},{9,5},{13,1},{2,14},{6,10},... | collective-permute-start | bytes 124424 | tf_op jit(solution)/shard_map/ppermute | solution.py:129
  104.0 11.7 %collective-permute-start.10 = (bf16[256,1024]{1,0:T(8,128)(2,1)}, bf16[256,1024]{1,0:T(8,128)(2,1)}, u32[]{:S(2)}, u32[]{:S(2)}) collective-permute-start(bf16[256,1024]{1,0:T(8,128)(2,1)} %slice.197), channel_id=1, source_target_pairs={{0,3},{1,2},{2,1},{3,0},{4,7},{5,6},{6,5},{7,4},{8,11},{9,10},{10,... | collective-permute-start | bytes 1572872 | tf_op jit(solution)/shard_map/ppermute | solution.py:37
  107.2 10.0 %collective-permute-start.9 = (bf16[256,1024]{1,0:T(8,128)(2,1)}, bf16[256,1024]{1,0:T(8,128)(2,1)}, u32[]{:S(2)}, u32[]{:S(2)}) collective-permute-start(bf16[256,1024]{1,0:T(8,128)(2,1)} %slice.196), channel_id=1, source_target_pairs={{0,1},{1,0},{2,3},{3,2},{4,5},{5,4},{6,7},{7,6},{8,9},{9,8},{10,11... | collective-permute-start | bytes 1572872 | tf_op jit(solution)/shard_map/ppermute | solution.py:37
  134.0 11.0 %collective-permute-start.15 = (f32[432,128]{1,0:T(8,128)S(1)}, f32[432,128]{1,0:T(8,128)S(1)}, u32[]{:S(2)}, u32[]{:S(2)}) collective-permute-start(f32[432,128]{1,0:T(8,128)S(1)} %get-tuple-element.80), channel_id=1, source_target_pairs={{0,96},{32,64},{64,32},{96,0},{1,97},{33,65},{65,33},{97,1},{2,98}... | collective-permute-start | bytes 663560 | tf_op jit(solution)/shard_map/ppermute | solution.py:143
  139.4 6.5 %collective-permute-start.17 = (f32[432,128]{1,0:T(8,128)S(1)}, f32[432,128]{1,0:T(8,128)S(1)}, u32[]{:S(2)}, u32[]{:S(2)}) collective-permute-start(f32[432,128]{1,0:T(8,128)S(1)} %get-tuple-element.81), channel_id=1, source_target_pairs={{0,32},{32,0},{64,96},{96,64},{1,33},{33,1},{65,97},{97,65},{2,34}... | collective-permute-start | bytes 663560 | tf_op jit(solution)/shard_map/ppermute | solution.py:144
  139.4 10.3 %collective-permute-start.19 = (f32[432,128]{1,0:T(8,128)S(1)}, f32[432,128]{1,0:T(8,128)S(1)}, u32[]{:S(2)}, u32[]{:S(2)}) collective-permute-start(f32[432,128]{1,0:T(8,128)S(1)} %get-tuple-element.74), channel_id=1, source_target_pairs={{0,96},{32,64},{64,32},{96,0},{1,97},{33,65},{65,33},{97,1},{2,98}... | collective-permute-start | bytes 663560 | tf_op jit(solution)/shard_map/ppermute | solution.py:143
  140.2 10.3 %collective-permute-start.21 = (f32[432,128]{1,0:T(8,128)S(1)}, f32[432,128]{1,0:T(8,128)S(1)}, u32[]{:S(2)}, u32[]{:S(2)}) collective-permute-start(f32[432,128]{1,0:T(8,128)S(1)} %get-tuple-element.75), channel_id=1, source_target_pairs={{0,32},{32,0},{64,96},{96,64},{1,33},{33,1},{65,97},{97,65},{2,34}... | collective-permute-start | bytes 663560 | tf_op jit(solution)/shard_map/ppermute | solution.py:144
  145.1 15.0 %collective-permute-start.16 = (f32[864,128]{1,0:T(8,128)S(1)}, f32[864,128]{1,0:T(8,128)S(1)}, u32[]{:S(2)}, u32[]{:S(2)}) collective-permute-start(f32[864,128]{1,0:T(8,128)S(1)} %pad_maximum_fusion.1), channel_id=1, source_target_pairs={{0,32},{32,0},{64,96},{96,64},{1,33},{33,1},{65,97},{97,65},{2,34}... | collective-permute-start | bytes 1327112 | tf_op jit(solution)/shard_map/ppermute | solution.py:148
  145.9 14.1 %collective-permute-start.18 = (f32[864,128]{1,0:T(8,128)S(1)}, f32[864,128]{1,0:T(8,128)S(1)}, u32[]{:S(2)}, u32[]{:S(2)}) collective-permute-start(f32[864,128]{1,0:T(8,128)S(1)} %pad_maximum_fusion.2), channel_id=1, source_target_pairs={{0,96},{32,64},{64,32},{96,0},{1,97},{33,65},{65,33},{97,1},{2,98}... | collective-permute-start | bytes 1327112 | tf_op jit(solution)/shard_map/ppermute | solution.py:148
  149.8 19.7 %collective-permute-start.20 = (f32[864,128]{1,0:T(8,128)S(1)}, f32[864,128]{1,0:T(8,128)S(1)}, u32[]{:S(2)}, u32[]{:S(2)}) collective-permute-start(f32[864,128]{1,0:T(8,128)S(1)} %pad_maximum_fusion.3), channel_id=1, source_target_pairs={{0,32},{32,0},{64,96},{96,64},{1,33},{33,1},{65,97},{97,65},{2,34}... | collective-permute-start | bytes 1327112 | tf_op jit(solution)/shard_map/ppermute | solution.py:148
  150.6 18.9 %collective-permute-start.22 = (f32[864,128]{1,0:T(8,128)S(1)}, f32[864,128]{1,0:T(8,128)S(1)}, u32[]{:S(2)}, u32[]{:S(2)}) collective-permute-start(f32[864,128]{1,0:T(8,128)S(1)} %pad_maximum_fusion.4), channel_id=1, source_target_pairs={{0,96},{32,64},{64,32},{96,0},{1,97},{33,65},{65,33},{97,1},{2,98}... | collective-permute-start | bytes 1327112 | tf_op jit(solution)/shard_map/ppermute | solution.py:148
  181.8 7.2 %collective-permute-start.27 = (bf16[208,128]{1,0:T(8,128)(2,1)S(1)}, bf16[208,128]{1,0:T(8,128)(2,1)S(1)}, u32[]{:S(2)}, u32[]{:S(2)}) collective-permute-start(bf16[208,128]{1,0:T(8,128)(2,1)S(1)} %concatenate.58), channel_id=1, source_target_pairs={{0,8},{4,12},{8,0},{12,4},{1,9},{5,13},{9,1},{13,5},{2,10},{6,14},... | collective-permute-start | bytes 159752 | tf_op jit(solution)/shard_map/ppermute | solution.py:175
  196.8 10.4 %all-to-all-start = ((bf16[8,16,1024]{2,1,0:T(8,128)(2,1)}), bf16[8,16,1024]{2,1,0:T(8,128)(2,1)S(1)}, u32[]{:S(2)}, u32[]{:S(2)}) async-start(bf16[8,16,1024]{2,1,0:T(8,128)(2,1)} %select_convert_fusion), calls=%async_computation | async-start | bytes 524288 | tf_op jit(solution)/shard_map/all_to_all | solution.py:201
  (16 other events, 275.9 us)
Sparse Core Ops, SparseCore 0:
  9.8 111.2 all-gather.2
